TPU v7x, 32 devices: a whole 2x2x4 slice. The times are simulated.
32 devices in a mesh: groups: 2 (over y), tile: 4 (over z), slab: 4 (over x, core).
Axes of the slice: x: 2, y: 2, z: 4, core: 2. Of those that a mesh axis runs over, the one named last changes fastest.
Arguments:
- phase_map: float32 [32, 512, 512], P(('groups', 'slab'), 'tile'), parts along dimension 0, may hold values from -3 to 3
- absorption: float32 [32, 512, 512], P(('groups', 'slab'), 'tile'), parts along dimension 0, may hold values from 0 to 0.1
- probe_wave: float32 [2, 128, 128], replicated, may hold values from -6 to 6
- measured: float32 [32, 128, 128], P(('groups', 'tile')), parts along dimension 0, may hold values from 0 to 2
- rows_at: int32 [32], P(('groups', 'tile')), parts along dimension 0, may hold values from 0 to 127
- cols_at: int32 [32], P(('groups', 'tile')), parts along dimension 0, may hold values from 0 to 384
- live_mask: int32 [32], P(('groups', 'tile')), parts along dimension 0, may hold values 0 or 1
Outputs:
- grad_phase: float32 [32, 512, 512], P(('groups', 'slab'), 'tile'), parts along dimension 0
- grad_absorption: float32 [32, 512, 512], P(('groups', 'slab'), 'tile'), parts along dimension 0
There are 2 independent parts, one for each index of `groups`. A program takes and returns all parts, laid end to end along the dimension named above; an argument that names none is the same for every part. Nothing has to cross between parts.
All inputs are finite; a program needn't handle non-finite values. No bound on the sum of `live_mask` on one device may be relied on, other than what follows from the above.
Results may differ from a plain program's by a relative error of at most 0.0003.
Values sent between devices are 32-bit elements; how exact they have to be, the bound alone decides.
A program may use at most 64 MiB of HBM per device.

v0:
```python
import math

import jax
import jax.numpy as jnp
from jax import lax
from jax.sharding import PartitionSpec as P

chirp_rate = 0.25
highest = lax.Precision.HIGHEST


def passed_along(array, axis, by):
    devices = lax.axis_size(axis)
    pairs = [(i, i + by) for i in range(devices) if 0 <= i + by < devices]
    return lax.ppermute(array, axis, pairs)


def tables(length):
    index = jnp.arange(length, dtype=jnp.int32)
    signed = jnp.where(index < length // 2, index, index - length).astype(jnp.float32)
    chirped = -jnp.pi * chirp_rate * signed * signed / length
    product = index[:, None] * index[None, :] % length
    rotation = 2.0 * jnp.pi * product.astype(jnp.float32) / length
    angles = chirped[:, None] + rotation
    kernel_real = jnp.sum(jnp.cos(angles), axis=0) / length
    kernel_imag = jnp.sum(jnp.sin(angles), axis=0) / length
    lagged = (index[:, None] - index[None, :]) % length
    norm_scale = 1.0 / math.sqrt(length)
    return (
        kernel_real[lagged],
        kernel_imag[lagged],
        jnp.cos(rotation) * norm_scale,
        -jnp.sin(rotation) * norm_scale,
    )


def make_blocks(mat_real, mat_imag, conj_sign):
    mat_other = conj_sign * mat_imag
    left_block = jnp.concatenate(
        [
            jnp.concatenate([mat_real, -mat_other], axis=1),
            jnp.concatenate([mat_other, mat_real], axis=1),
        ],
        axis=0,
    )
    right_block = jnp.concatenate(
        [
            jnp.concatenate([mat_real, mat_other], axis=1),
            jnp.concatenate([-mat_other, mat_real], axis=1),
        ],
        axis=0,
    )
    return (left_block, right_block)


def sandwich(blocks, wave_real, wave_imag):
    left_block, right_block = blocks
    side = wave_real.shape[1]
    stacked = jnp.concatenate([wave_real, wave_imag], axis=1)
    left = jnp.einsum("ij,bjk->bik", left_block, stacked, precision=highest)
    beside = jnp.concatenate([left[:, :side], left[:, side:]], axis=2)
    result = jnp.einsum("bij,jk->bik", beside, right_block, precision=highest)
    return (result[:, :, :side], result[:, :, side:])


def cut_columns(target, starts, window_side):

    def single(start_col):
        anchor = jnp.zeros((), jnp.int32)
        return lax.dynamic_slice(
            target, (anchor, anchor, start_col), (target.shape[0], target.shape[1], window_side)
        )

    return jax.vmap(single)(starts)


def cut_rows(stacked, starts, window_side):

    def single(portion, start_row):
        anchor = jnp.zeros((), jnp.int32)
        return lax.dynamic_slice(
            portion, (anchor, start_row, anchor), (portion.shape[0], window_side, portion.shape[2])
        )

    return jax.vmap(single)(stacked, starts)


def place_rows(pieces, starts, window_side):

    def single(portion, start_row):
        anchor = jnp.zeros((), jnp.int32)
        canvas = jnp.zeros((portion.shape[0], 2 * window_side, portion.shape[2]), portion.dtype)
        return lax.dynamic_update_slice(canvas, portion, (anchor, start_row, anchor))

    return jax.vmap(single)(pieces, starts)


def add_columns(targets, pieces, starts):
    window_side = pieces[0].shape[3]

    def deposit(slot_index, current):
        anchor = jnp.zeros((), jnp.int32)
        corner = (anchor, anchor, starts[slot_index])
        result = []
        for target, portion in zip(current, pieces):
            before = lax.dynamic_slice(
                target, corner, (target.shape[0], target.shape[1], window_side)
            )
            result.append(lax.dynamic_update_slice(target, before + portion[slot_index], corner))
        return tuple(result)

    return lax.fori_loop(0, starts.shape[0], deposit, targets)


def keep_active(buffer, values, lead_index, active):
    current = lax.dynamic_slice_in_dim(buffer, lead_index, values.shape[0], 0)
    return lax.dynamic_update_slice_in_dim(
        buffer, jnp.where(active, values, current), lead_index, 0
    )


def local(phase_map, absorption, probe_wave, measured, rows_at, cols_at, live_mask):
    layers = phase_map.shape[0]
    window_side = probe_wave.shape[2]
    windows = measured.shape[0]
    slab_count = lax.axis_size("slab")
    position = lax.axis_index("slab")
    spread_real, spread_imag, fourier_real, fourier_imag = tables(window_side)
    spread_fwd = make_blocks(spread_real, spread_imag, 1.0)
    spread_adj = make_blocks(spread_real, spread_imag, -1.0)
    fourier_fwd = make_blocks(fourier_real, fourier_imag, 1.0)
    fourier_adj = make_blocks(fourier_real, fourier_imag, -1.0)
    upper_phase = cut_columns(phase_map, cols_at, window_side)
    upper_absorb = cut_columns(absorption, cols_at, window_side)
    below_phase, below_absorb = passed_along((phase_map, absorption), "tile", -1)
    lower_phase = cut_columns(below_phase, cols_at, window_side)
    lower_absorb = cut_columns(below_absorb, cols_at, window_side)
    patch_phase = cut_rows(
        jnp.concatenate([upper_phase, lower_phase], axis=2), rows_at, window_side
    )
    patch_absorb = cut_rows(
        jnp.concatenate([upper_absorb, lower_absorb], axis=2), rows_at, window_side
    )
    damping = jnp.exp(-patch_absorb)
    trans_real = damping * jnp.cos(patch_phase)
    trans_imag = damping * jnp.sin(patch_phase)
    group_size = 1
    blocks = windows // group_size
    turn_count = blocks + slab_count - 1
    start_wave = probe_wave[None]
    store_shape = (windows, layers, window_side, window_side)

    def forward_turn(turn_index, carried):
        incoming, entered_real, entered_imag, leaving_all = carried
        block_index = turn_index - position
        active = (block_index >= 0) & (block_index < blocks)
        lead_index = jnp.clip(block_index, 0, blocks - 1) * group_size
        current = jnp.where(position == 0, start_wave, incoming)
        wave_real = current[:, 0]
        wave_imag = current[:, 1]
        local_real = lax.dynamic_slice_in_dim(trans_real, lead_index, group_size, 0)
        local_imag = lax.dynamic_slice_in_dim(trans_imag, lead_index, group_size, 0)
        seen_real = []
        seen_imag = []
        for layer_index in range(layers):
            seen_real.append(wave_real)
            seen_imag.append(wave_imag)
            mixed_real = (
                local_real[:, layer_index] * wave_real - local_imag[:, layer_index] * wave_imag
            )
            mixed_imag = (
                local_real[:, layer_index] * wave_imag + local_imag[:, layer_index] * wave_real
            )
            wave_real, wave_imag = sandwich(spread_fwd, mixed_real, mixed_imag)
        entered_real = keep_active(entered_real, jnp.stack(seen_real, axis=1), lead_index, active)
        entered_imag = keep_active(entered_imag, jnp.stack(seen_imag, axis=1), lead_index, active)
        leaving = jnp.stack([wave_real, wave_imag], axis=1)
        leaving_all = keep_active(leaving_all, leaving, lead_index, active)
        incoming = passed_along(leaving, "slab", 1)
        return (incoming, entered_real, entered_imag, leaving_all)

    forward_start = (
        jnp.zeros_like(start_wave),
        jnp.zeros(store_shape, jnp.float32),
        jnp.zeros(store_shape, jnp.float32),
        jnp.zeros((windows,) + probe_wave.shape, jnp.float32),
    )
    unused_wave, entered_real, entered_imag, leaving_all = lax.fori_loop(
        0, turn_count, forward_turn, forward_start
    )
    weights = live_mask.astype(jnp.float32)[:, None, None]

    def far_side(exits):
        far_real, far_imag = sandwich(fourier_fwd, exits[:, 0], exits[:, 1])
        excess = 0.5 * weights * (far_real * far_real + far_imag * far_imag - measured)
        back_real, back_imag = sandwich(fourier_adj, excess * far_real, excess * far_imag)
        return jnp.stack([back_real, back_imag], axis=1)

    def no_side(exits):
        return jnp.zeros_like(exits)

    seeds = lax.cond(position == slab_count - 1, far_side, no_side, leaving_all)

    def backward_turn(turn_index, carried):
        incoming, grads_real, grads_imag = carried
        block_index = turn_index - (slab_count - 1 - position)
        active = (block_index >= 0) & (block_index < blocks)
        lead_index = jnp.clip(block_index, 0, blocks - 1) * group_size
        seed_now = lax.dynamic_slice_in_dim(seeds, lead_index, group_size, 0)
        current = jnp.where(position == slab_count - 1, seed_now, incoming)
        back_real = current[:, 0]
        back_imag = current[:, 1]
        local_real = lax.dynamic_slice_in_dim(trans_real, lead_index, group_size, 0)
        local_imag = lax.dynamic_slice_in_dim(trans_imag, lead_index, group_size, 0)
        seen_real = lax.dynamic_slice_in_dim(entered_real, lead_index, group_size, 0)
        seen_imag = lax.dynamic_slice_in_dim(entered_imag, lead_index, group_size, 0)
        found_real = [None] * layers
        found_imag = [None] * layers
        for layer_index in reversed(range(layers)):
            mixed_real, mixed_imag = sandwich(spread_adj, back_real, back_imag)
            wave_real = seen_real[:, layer_index]
            wave_imag = seen_imag[:, layer_index]
            found_real[layer_index] = wave_real * mixed_real + wave_imag * mixed_imag
            found_imag[layer_index] = wave_real * mixed_imag - wave_imag * mixed_real
            factor_real = local_real[:, layer_index]
            factor_imag = local_imag[:, layer_index]
            back_real = factor_real * mixed_real + factor_imag * mixed_imag
            back_imag = factor_real * mixed_imag - factor_imag * mixed_real
        grads_real = keep_active(grads_real, jnp.stack(found_real, axis=1), lead_index, active)
        grads_imag = keep_active(grads_imag, jnp.stack(found_imag, axis=1), lead_index, active)
        incoming = passed_along(jnp.stack([back_real, back_imag], axis=1), "slab", -1)
        return (incoming, grads_real, grads_imag)

    backward_start = (
        jnp.zeros_like(start_wave),
        jnp.zeros(store_shape, jnp.float32),
        jnp.zeros(store_shape, jnp.float32),
    )
    unused_back, grads_real, grads_imag = lax.fori_loop(
        0, turn_count, backward_turn, backward_start
    )
    d_phase = grads_imag * trans_real - grads_real * trans_imag
    d_absorb = -(grads_real * trans_real + grads_imag * trans_imag)
    placed_phase = place_rows(d_phase, rows_at, window_side)
    placed_absorb = place_rows(d_absorb, rows_at, window_side)
    empty_pair = (jnp.zeros_like(phase_map), jnp.zeros_like(absorption))
    own_pair = add_columns(
        empty_pair, (placed_phase[:, :, :window_side], placed_absorb[:, :, :window_side]), cols_at
    )
    spill_phase = placed_phase[:, :, window_side:]
    spill_absorb = placed_absorb[:, :, window_side:]
    spill_pair = add_columns(empty_pair, (spill_phase, spill_absorb), cols_at)
    from_above = passed_along((spill_pair[0], spill_pair[1]), "tile", 1)
    return (own_pair[0] + from_above[0], own_pair[1] + from_above[1])


def solution(mesh):
    return jax.shard_map(
        local,
        mesh=mesh,
        in_specs=(
            P(("groups", "slab"), "tile", None),
            P(("groups", "slab"), "tile", None),
            P(),
            P(("groups", "tile"), None, None),
            P(("groups", "tile")),
            P(("groups", "tile")),
            P(("groups", "tile")),
        ),
        out_specs=(P(("groups", "slab"), "tile", None), P(("groups", "slab"), "tile", None)),
        check_vma=False,
    )
```

profile of v0, /device:TPU:19, one launch (start us, length us, event | category | flops | bytes accessed | tf_op | source)
XLA Modules:
  0.0 629.8 jit_solution(16645484128072765107)
XLA Ops:
  2.3 2.1 collective-permute-start.3
  4.4 2.5 copy.36
  6.9 2.1 collective-permute-start.2
  10.1 2.1 gather_fusion.2
  12.2 3.3 gather_fusion
  15.6 97.2 %gather_fusion.5 = f32[16384]{0:T(1024)S(1)} fusion(f32[128]{0:T(128)S(1)} %get-tuple-element.1072, s32[16384]{0:T(1024)S(1)} %fusion.87), kind=kCustom, calls=%fused_computation.5 | custom fusion | bytes 196608 | tf_op jit(solution)/shard_map/gather | solution.py:31
  112.8 97.2 %gather_fusion.4 = f32[16384]{0:T(1024)S(1)} fusion(f32[128]{0:T(128)S(1)} %get-tuple-element.1073, s32[16384]{0:T(1024)S(1)} %fusion.87), kind=kCustom, calls=%fused_computation.4 | custom fusion | bytes 196608 | tf_op jit(solution)/shard_map/gather | solution.py:30
  211.5 2.1 gather_fusion.3
  213.6 2.0 pad_maximum_fusion.4
  215.6 2.6 copy.41
  218.2 3.3 gather_fusion.1
  221.5 2.0 pad_maximum_fusion.3
  223.5 2.5 copy.38
  226.0 3.9 gather_fusion.7
  230.0 2.2 gather_fusion.6
  232.1 4.9 sine_multiply_fusion
  240.6 112.2 %while.71 = (s32[]{:T(128)}, f32[1,2,128,128]{3,2,1,0:T(8,128)S(1)}, f32[4,4,128,128]{3,2,1,0:T(8,128)S(1)}, f32[4,4,128,128]{3,2,1,0:T(8,128)S(1)}, f32[4,2,128...) while((s32[]{:T(128)}, ...), condition=%wide.region_3.4_spmd, body=%wide.region_2.3_spmd.sunk | while | flops 806584320 | bytes 10617177 | solution.py:188
  266.8 4.2 collective-permute-done
  283.2 4.2 collective-permute-done
  299.5 4.2 collective-permute-done
  315.9 4.2 collective-permute-done
  332.2 4.2 collective-permute-done
  348.6 4.2 collective-permute-done
  352.7 6.5 %conditional.1 = (f32[4,2,128,128]{3,2,1,0:T(8,128)}) conditional(s32[]{:T(128)} %convert_element_type.52, () %tuple.81, (f32[4]{0:T(128)S(1)}, f32[4,2,128,128]{3,2,1,0:T(8,128)}, f32[256,256]{1,0:T(8,128)}, f32[256,256]{1,0:T(8,128)}, f32[4,128,128]{2,1,0:T(8,128)}, /*index=5*/f32[256,256]{1,0:T(8,128)}, f32[256,256]{1,0:T(8,128)}) %tuple.83), branch_computations={%region_4.5_spmd, %region_5.6_spmd} | conditional | flops 1611726848 | bytes 19136708 | solution.py:202
  362.1 106.6 %while.72 = (s32[]{:T(128)}, f32[1,2,128,128]{3,2,1,0:T(8,128)}, f32[4,4,128,128]{3,1,2,0:T(4,128)}, f32[4,4,128,128]{3,1,2,0:T(4,128)}, s32[]{:T(128)}, /*index...) while((s32[]{:T(128)}, f32[1,2,128,128]{3,2,1,0:T(8,128)}, ...), condition=%wide.region_7.8_spmd, body=%wide.region_6.7_spmd.sunk | while | flops 806944768 | bytes 13369717 | solution.py:239
  370.6 1.9 collective-permute-start.1
  385.8 1.9 collective-permute-start.1
  401.0 1.9 collective-permute-start.1
  416.3 1.9 collective-permute-start.1
  431.5 1.9 collective-permute-start.1
  446.7 1.9 collective-permute-start.1
  461.9 1.9 collective-permute-start.1
  468.6 3.4 add_negate_fusion
  472.7 34.5 %while.76 = (s32[]{:T(128)}, f32[4,4,256,128]{3,2,1,0:T(8,128)S(1)}, s32[4,4]{1,0:T(4,128)S(1)}, f32[4,4,128,128]{3,1,2,0:T(4,128)}, s32[]{:T(128)}, /*index=5*/s32[4]{0:T(128)S(1)}, s32[]{:T(128)}) while((s32[]{:T(128)}, f32[4,4,256,128]{3,2,1,0:T(8,128)S(1)}, s32[4,4]{1,0:T(4,128)S(1)}, f32[4,4,128,128]{3,1,2,0:T(4,128)}, s32[]{:T(128)}, ...), condition=%wide.while_cond.1, body=%wide.while_body.1.sunk | while | flops 65565 | bytes 1835203 | solution.py:93
  473.4 3.3 and_reduce_fusion.5
  482.0 3.3 and_reduce_fusion.5
  488.0 1.9 dynamic-update-slice.7
  490.6 3.3 and_reduce_fusion.5
  496.7 1.9 dynamic-update-slice.7
  499.3 3.3 and_reduce_fusion.5
  508.9 31.4 %while.75 = (s32[]{:T(128)}, f32[4,4,256,128]{3,2,1,0:T(8,128)S(1)}, s32[4,4]{1,0:T(4,128)S(1)}, f32[4,4,128,128]{3,1,2,0:T(4,128)S(1)}, s32[]{:T(128)}, /*index=5*/s32[4]{0:T(128)S(1)}, s32[]{:T(128)}) while((s32[]{:T(128)}, f32[4,4,256,128]{3,2,1,0:T(8,128)S(1)}, s32[4,4]{1,0:T(4,128)S(1)}, f32[4,4,128,128]{3,1,2,0:T(4,128)S(1)}, s32[]{:T(128)}, ...), condition=%wide.while_cond, body=%wide.while_body.sunk | while | flops 65565 | bytes 1835203 | solution.py:93
  509.5 3.3 and_reduce_fusion.4
  512.9 2.0 copy_select_fusion.4
  517.4 3.3 and_reduce_fusion.4
  520.7 2.0 copy_select_fusion.4
  522.7 1.9 dynamic-update-slice.6
  525.3 3.3 and_reduce_fusion.4
  528.6 2.0 copy_select_fusion.4
  530.6 1.9 dynamic-update-slice.6
  533.1 3.3 and_reduce_fusion.4
  536.5 2.0 copy_select_fusion.4
  543.6 33.3 %while.74 = (s32[]{:T(128)}, f32[4,128,512]{2,1,0:T(8,128)}, f32[4,128,512]{2,1,0:T(8,128)}, s32[4]{0:T(128)S(1)}, f32[4,4,128,128]{3,2,1,0:T(8,128)S(1)}, /*ind...) while((s32[]{:T(128)}, f32[4,128,512]{2,1,0:T(8,128)}, f32[4,128,512]{2,1,0:T(8,128)}, ...), condition=%wide.region_13.14_spmd, body=%wide.region_12.13_spmd.sunk | while | flops 131077 | bytes 2621595 | solution.py:112
  554.3 2.6 dynamic_update_slice.88
  556.8 2.5 dynamic_update_slice.87
  563.1 2.6 dynamic_update_slice.88
  565.6 2.5 dynamic_update_slice.87
  571.9 2.6 dynamic_update_slice.88
  574.5 2.5 dynamic_update_slice.87
  577.0 5.9 collective-permute-start.5
  582.9 1.9 collective-permute-start.4
  585.1 25.7 %while.73 = (s32[]{:T(128)}, f32[4,128,512]{2,1,0:T(8,128)S(1)}, f32[4,128,512]{2,1,0:T(8,128)S(1)}, s32[4]{0:T(128)S(1)}, f32[4,4,128,128]{3,2,1,0:T(8,128)}, /...) while((s32[]{:T(128)}, f32[4,128,512]{2,1,0:T(8,128)S(1)}, ...), condition=%wide.region_11.12_spmd, body=%wide.region_10.11_spmd.sunk | while | flops 131077 | bytes 2621595 | solution.py:112
  610.9 2.4 add.385
  613.3 14.1 %collective-permute-done.4 = f32[4,128,512]{2,1,0:T(8,128)} collective-permute-done((f32[4,128,512]{2,1,0:T(8,128)}, f32[4,128,512]{2,1,0:T(8,128)}, u32[]{:S(2)}, u32[]{:S(2)}) %collective-permute-start.4) | collective-permute-done | bytes 1048608 | tf_op jit(solution)/shard_map/ppermute | solution.py:15
  627.4 2.4 add.384
  (467 shorter events, 253.8 us)
Async XLA Ops:
  0.6 9.2 %copy-start.9 = (s32[3]{0:T(128)S(1)}, s32[3]{0:T(128)}, u32[]{:S(2)}) copy-start(s32[3]{0:T(128)} %constant.192.clone.1) | copy-start | bytes 40
  0.6 9.1 %copy-start.12 = (s32[4]{0:T(128)S(1)}, s32[4]{0:T(128)}, u32[]{:S(2)}) copy-start(s32[4]{0:T(128)} %param.22) | copy-start | bytes 52
  0.7 9.1 %copy-start.11 = (s32[4]{0:T(128)S(1)}, s32[4]{0:T(128)}, u32[]{:S(2)}) copy-start(s32[4]{0:T(128)} %param.21) | copy-start | bytes 52
  2.3 209.2 %collective-permute-start.3 = (f32[4,128,512]{1,0,2:T(4,128)S(1)}, f32[4,128,512]{1,0,2:T(4,128)S(1)}, u32[]{:S(2)}, u32[]{:S(2)}) collective-permute-start(f32[4,128,512]{1,0,2:T(4,128)S(1)} %copy.39), channel_id=1, source_target_pairs={{4,0},{8,4},{12,8},{5,1},{9,5},{13,9},{6,2},{10,6},{14,10},{7,3},{... | collective-permute-start | bytes 3145736 | tf_op jit(solution)/shard_map/ppermute | solution.py:15
  6.9 211.2 %collective-permute-start.2 = (f32[4,128,512]{1,0,2:T(4,128)}, f32[4,128,512]{1,0,2:T(4,128)}, u32[]{:S(2)}, u32[]{:S(2)}) collective-permute-start(f32[4,128,512]{1,0,2:T(4,128)} %copy.36), channel_id=1, source_target_pairs={{4,0},{8,4},{12,8},{5,1},{9,5},{13,9},{6,2},{10,6},{14,10},{7,3},{... | collective-permute-start | bytes 3145736 | tf_op jit(solution)/shard_map/ppermute | solution.py:15
  112.8 97.2 %copy-start.10 = (s32[4]{0:T(128)S(1)}, s32[4]{0:T(128)}, u32[]{:S(2)}) copy-start(s32[4]{0:T(128)} %param.23) | copy-start | bytes 52
  226.0 3.9 copy-start.2
  237.1 2.4 copy-start
  237.1 2.4 copy-start.1
  250.5 4.2 collective-permute-start
  264.5 6.5 %collective-permute-start = (f32[1,2,128,128]{3,2,1,0:T(8,128)}, f32[1,2,128,128]{3,2,1,0:T(8,128)S(1)}, u32[]{:S(2)}, u32[]{:S(2)}) collective-permute-start(f32[1,2,128,128]{3,2,1,0:T(8,128)} %get-tuple-element.1413), channel_id=1, source_target_pairs={{0,1},{1,2},{2,3},{4,5},{5,6},{6,7},{8,9},{9,10},{10,11},{12,13},{... | collective-permute-start | bytes 393224 | tf_op jit(solution)/shard_map/while/body/eval_jaxpr/ppermute | solution.py:15
  280.9 6.5 %collective-permute-start = (f32[1,2,128,128]{3,2,1,0:T(8,128)}, f32[1,2,128,128]{3,2,1,0:T(8,128)S(1)}, u32[]{:S(2)}, u32[]{:S(2)}) collective-permute-start(f32[1,2,128,128]{3,2,1,0:T(8,128)} %get-tuple-element.1413), channel_id=1, source_target_pairs={{0,1},{1,2},{2,3},{4,5},{5,6},{6,7},{8,9},{9,10},{10,11},{12,13},{... | collective-permute-start | bytes 393224 | tf_op jit(solution)/shard_map/while/body/eval_jaxpr/ppermute | solution.py:15
  297.2 6.5 %collective-permute-start = (f32[1,2,128,128]{3,2,1,0:T(8,128)}, f32[1,2,128,128]{3,2,1,0:T(8,128)S(1)}, u32[]{:S(2)}, u32[]{:S(2)}) collective-permute-start(f32[1,2,128,128]{3,2,1,0:T(8,128)} %get-tuple-element.1413), channel_id=1, source_target_pairs={{0,1},{1,2},{2,3},{4,5},{5,6},{6,7},{8,9},{9,10},{10,11},{12,13},{... | collective-permute-start | bytes 393224 | tf_op jit(solution)/shard_map/while/body/eval_jaxpr/ppermute | solution.py:15
  313.6 6.5 %collective-permute-start = (f32[1,2,128,128]{3,2,1,0:T(8,128)}, f32[1,2,128,128]{3,2,1,0:T(8,128)S(1)}, u32[]{:S(2)}, u32[]{:S(2)}) collective-permute-start(f32[1,2,128,128]{3,2,1,0:T(8,128)} %get-tuple-element.1413), channel_id=1, source_target_pairs={{0,1},{1,2},{2,3},{4,5},{5,6},{6,7},{8,9},{9,10},{10,11},{12,13},{... | collective-permute-start | bytes 393224 | tf_op jit(solution)/shard_map/while/body/eval_jaxpr/ppermute | solution.py:15
  329.9 6.5 %collective-permute-start = (f32[1,2,128,128]{3,2,1,0:T(8,128)}, f32[1,2,128,128]{3,2,1,0:T(8,128)S(1)}, u32[]{:S(2)}, u32[]{:S(2)}) collective-permute-start(f32[1,2,128,128]{3,2,1,0:T(8,128)} %get-tuple-element.1413), channel_id=1, source_target_pairs={{0,1},{1,2},{2,3},{4,5},{5,6},{6,7},{8,9},{9,10},{10,11},{12,13},{... | collective-permute-start | bytes 393224 | tf_op jit(solution)/shard_map/while/body/eval_jaxpr/ppermute | solution.py:15
  346.3 6.5 %collective-permute-start = (f32[1,2,128,128]{3,2,1,0:T(8,128)}, f32[1,2,128,128]{3,2,1,0:T(8,128)S(1)}, u32[]{:S(2)}, u32[]{:S(2)}) collective-permute-start(f32[1,2,128,128]{3,2,1,0:T(8,128)} %get-tuple-element.1413), channel_id=1, source_target_pairs={{0,1},{1,2},{2,3},{4,5},{5,6},{6,7},{8,9},{9,10},{10,11},{12,13},{... | collective-permute-start | bytes 393224 | tf_op jit(solution)/shard_map/while/body/eval_jaxpr/ppermute | solution.py:15
  352.7 1.4 copy-start.5
  354.0 1.0 copy-start.6
  354.1 1.9 copy-start.7
  354.7 1.4 copy-start.4
  356.0 1.2 copy-start.3
  370.6 6.7 %collective-permute-start.1 = (f32[1,2,128,128]{3,2,1,0:T(8,128)}, f32[1,2,128,128]{3,2,1,0:T(8,128)}, u32[]{:S(2)}, u32[]{:S(2)}) collective-permute-start(f32[1,2,128,128]{3,2,1,0:T(8,128)} %pad_maximum_fusion.22), channel_id=1, source_target_pairs={{1,0},{2,1},{3,2},{5,4},{6,5},{7,6},{9,8},{10,9},{11,10},{13,12},{... | collective-permute-start | bytes 393224 | tf_op jit(solution)/shard_map/while/body/eval_jaxpr/ppermute | solution.py:15
  385.8 6.7 %collective-permute-start.1 = (f32[1,2,128,128]{3,2,1,0:T(8,128)}, f32[1,2,128,128]{3,2,1,0:T(8,128)}, u32[]{:S(2)}, u32[]{:S(2)}) collective-permute-start(f32[1,2,128,128]{3,2,1,0:T(8,128)} %pad_maximum_fusion.22), channel_id=1, source_target_pairs={{1,0},{2,1},{3,2},{5,4},{6,5},{7,6},{9,8},{10,9},{11,10},{13,12},{... | collective-permute-start | bytes 393224 | tf_op jit(solution)/shard_map/while/body/eval_jaxpr/ppermute | solution.py:15
  401.0 6.7 %collective-permute-start.1 = (f32[1,2,128,128]{3,2,1,0:T(8,128)}, f32[1,2,128,128]{3,2,1,0:T(8,128)}, u32[]{:S(2)}, u32[]{:S(2)}) collective-permute-start(f32[1,2,128,128]{3,2,1,0:T(8,128)} %pad_maximum_fusion.22), channel_id=1, source_target_pairs={{1,0},{2,1},{3,2},{5,4},{6,5},{7,6},{9,8},{10,9},{11,10},{13,12},{... | collective-permute-start | bytes 393224 | tf_op jit(solution)/shard_map/while/body/eval_jaxpr/ppermute | solution.py:15
  416.3 6.7 %collective-permute-start.1 = (f32[1,2,128,128]{3,2,1,0:T(8,128)}, f32[1,2,128,128]{3,2,1,0:T(8,128)}, u32[]{:S(2)}, u32[]{:S(2)}) collective-permute-start(f32[1,2,128,128]{3,2,1,0:T(8,128)} %pad_maximum_fusion.22), channel_id=1, source_target_pairs={{1,0},{2,1},{3,2},{5,4},{6,5},{7,6},{9,8},{10,9},{11,10},{13,12},{... | collective-permute-start | bytes 393224 | tf_op jit(solution)/shard_map/while/body/eval_jaxpr/ppermute | solution.py:15
  431.5 6.7 %collective-permute-start.1 = (f32[1,2,128,128]{3,2,1,0:T(8,128)}, f32[1,2,128,128]{3,2,1,0:T(8,128)}, u32[]{:S(2)}, u32[]{:S(2)}) collective-permute-start(f32[1,2,128,128]{3,2,1,0:T(8,128)} %pad_maximum_fusion.22), channel_id=1, source_target_pairs={{1,0},{2,1},{3,2},{5,4},{6,5},{7,6},{9,8},{10,9},{11,10},{13,12},{... | collective-permute-start | bytes 393224 | tf_op jit(solution)/shard_map/while/body/eval_jaxpr/ppermute | solution.py:15
  446.7 6.7 %collective-permute-start.1 = (f32[1,2,128,128]{3,2,1,0:T(8,128)}, f32[1,2,128,128]{3,2,1,0:T(8,128)}, u32[]{:S(2)}, u32[]{:S(2)}) collective-permute-start(f32[1,2,128,128]{3,2,1,0:T(8,128)} %pad_maximum_fusion.22), channel_id=1, source_target_pairs={{1,0},{2,1},{3,2},{5,4},{6,5},{7,6},{9,8},{10,9},{11,10},{13,12},{... | collective-permute-start | bytes 393224 | tf_op jit(solution)/shard_map/while/body/eval_jaxpr/ppermute | solution.py:15
  461.9 6.7 %collective-permute-start.1 = (f32[1,2,128,128]{3,2,1,0:T(8,128)}, f32[1,2,128,128]{3,2,1,0:T(8,128)}, u32[]{:S(2)}, u32[]{:S(2)}) collective-permute-start(f32[1,2,128,128]{3,2,1,0:T(8,128)} %pad_maximum_fusion.22), channel_id=1, source_target_pairs={{1,0},{2,1},{3,2},{5,4},{6,5},{7,6},{9,8},{10,9},{11,10},{13,12},{... | collective-permute-start | bytes 393224 | tf_op jit(solution)/shard_map/while/body/eval_jaxpr/ppermute | solution.py:15
  472.0 0.7 copy-start.8
  577.0 33.9 %collective-permute-start.5 = (f32[4,128,512]{2,1,0:T(8,128)}, f32[4,128,512]{2,1,0:T(8,128)}, u32[]{:S(2)}, u32[]{:S(2)}) collective-permute-start(f32[4,128,512]{2,1,0:T(8,128)} %get-tuple-element.771), channel_id=1, source_target_pairs={{0,4},{4,8},{8,12},{1,5},{5,9},{9,13},{2,6},{6,10},{10,14},{3,7},{... | collective-permute-start | bytes 3145736 | tf_op jit(solution)/shard_map/ppermute | solution.py:15
  582.9 44.5 %collective-permute-start.4 = (f32[4,128,512]{2,1,0:T(8,128)}, f32[4,128,512]{2,1,0:T(8,128)}, u32[]{:S(2)}, u32[]{:S(2)}) collective-permute-start(f32[4,128,512]{2,1,0:T(8,128)} %get-tuple-element.769), channel_id=1, source_target_pairs={{0,4},{4,8},{8,12},{1,5},{5,9},{9,13},{2,6},{6,10},{10,14},{3,7},{... | collective-permute-start | bytes 3145736 | tf_op jit(solution)/shard_map/ppermute | solution.py:15
where the time goes:
time: 637 us; the launch traced here: 630 us
  local copies, waits for them, and re-layouts  315 us (49%)
  other arithmetic  173 us (27%)
  matrix products  47.7 us (7%)
  waiting for transfers between devices  41 us (6%)
  starting transfers between devices  34.5 us (5%)
  loops' own time  17.3 us (3%)
    gather x1, local copies, waits for them, and re-layouts, tables(): kernel_real[lagged]  97.2 us
    gather x1, local copies, waits for them, and re-layouts, tables(): kernel_imag[lagged]  97.2 us
    scatter x16, other arithmetic  41.5 us
    ppermute x18, waiting for transfers between devices, passed_along(): return lax.ppermute(array, axis, pairs)  41 us
    ppermute x18, starting transfers between devices, passed_along(): return lax.ppermute(array, axis, pairs)  34.5 us
    sub x28, other arithmetic, forward_turn(): local_real[:, layer_index] * wave_real  34.3 us
    dynamic_update_slice x16, local copies, waits for them, and re-layouts, deposit(): lax.dynamic_update_slice(target, before + portion[slot_index], corner)  28.7 us
    scatter x32, local copies, waits for them, and re-layouts  24.1 us
  transfers between devices with their start and end apart: 18, of which 8 were waited for; matrix products, arithmetic and copies ran while one was open for 43% of the time, Pallas kernels for 0%

commit v1 on v0

v1 whole, which is shorter than its diff:
```python
import functools
import math

import jax
import jax.numpy as jnp
import ml_dtypes
import numpy as np
from jax import lax
from jax.experimental import pallas as pl
from jax.experimental.pallas import tpu as pltpu
from jax.sharding import PartitionSpec as P

chirp_rate = 0.25
vmem_limit = 56 * 1024 * 1024


def split_host(mat):
    high = mat.astype(np.float32).astype(ml_dtypes.bfloat16)
    low = (mat - high.astype(np.float64)).astype(np.float32).astype(ml_dtypes.bfloat16)
    return high, low


def tables(length):
    index = np.arange(length)
    signed = np.where(index < length // 2, index, index - length).astype(np.float64)
    chirped = -np.pi * chirp_rate * signed * signed / length
    rotation = 2.0 * np.pi * (index[:, None] * index[None, :] % length) / length
    kernel = np.exp(1j * (chirped[:, None] + rotation)).sum(axis=0) / length
    spread = kernel[(index[:, None] - index[None, :]) % length]
    fourier = np.exp(-1j * rotation) / math.sqrt(length)
    forms = []
    for mat in (spread, fourier):
        re, im = mat.real, mat.imag
        minus = np.block([[re, im], [-im, re]])
        plus = np.block([[re, -im], [im, re]])
        for block in (minus, plus):
            high, low = split_host(block)
            forms.append(
                (np.concatenate([high, high, low], axis=0), np.concatenate([high, high, low], axis=1))
            )
    (q_minus, q_plus, f_minus, f_plus) = forms
    return (
        q_plus[1], q_minus[0], q_minus[1], q_plus[0],
        f_plus[1], f_minus[0], f_minus[1], f_plus[0],
    )


def halves(array):
    high = array.astype(jnp.bfloat16)
    low = (array - high.astype(jnp.float32)).astype(jnp.bfloat16)
    return high, low


def sandwich(left_ref, right_ref, wave_real, wave_imag):
    side = wave_real.shape[0]
    high, low = halves(jnp.concatenate([wave_real, wave_imag], axis=1))
    beside = jnp.dot(
        jnp.concatenate([high, low, high], axis=1), right_ref[...],
        preferred_element_type=jnp.float32,
    )
    high, low = halves(jnp.concatenate([beside[:, :side], beside[:, side:]], axis=0))
    stacked = jnp.dot(
        left_ref[...], jnp.concatenate([high, low, high], axis=0),
        preferred_element_type=jnp.float32,
    )
    return stacked[:side], stacked[side:]


def cos_sin(angle):
    turns = jnp.floor(angle * (2.0 / math.pi) + 0.5)
    rest = angle - turns * 1.5703125
    rest = rest - turns * 4.837512969970703e-4
    rest = rest - turns * 7.549789948768648e-8
    sq = rest * rest
    sin_part = rest + rest * sq * (-1.6666654611e-1 + sq * (8.3321608736e-3 + sq * -1.9515295891e-4))
    cos_part = 1.0 - 0.5 * sq + sq * sq * (
        4.166664568298827e-2 + sq * (-1.388731625493765e-3 + sq * 2.443315711809948e-5)
    )
    half = jnp.floor(turns * 0.5)
    odd = (turns - 2.0 * half) > 0.5
    flip = 1.0 - 2.0 * (half - 2.0 * jnp.floor(half * 0.5))
    cos_out = jnp.where(odd, -sin_part, cos_part) * flip
    sin_out = jnp.where(odd, cos_part, sin_part) * flip
    return cos_out, sin_out


def column_base(col, side, cols):
    return pl.multiple_of(jnp.minimum(col // side, cols // side - 2) * side, side)


def cut_kernel(rows_ref, cols_ref, phase_ref, absorb_ref, below_phase_ref, below_absorb_ref, out_ref, tall):
    window, layers, _, side, _ = out_ref.shape
    cols = phase_ref.shape[2]
    for layer in range(layers):
        for which, (upper, lower) in enumerate(
            ((phase_ref, below_phase_ref), (absorb_ref, below_absorb_ref))
        ):
            tall[layer, which, :side] = upper[layer]
            tall[layer, which, side:] = lower[layer]

    def one(w, carried):
        row, col = rows_ref[w], cols_ref[w]
        base = column_base(col, side, cols)
        shift = lax.rem(2 * side - (col - base), 2 * side)
        top = pl.multiple_of(row // 8 * 8, 8)
        lift = lax.rem(side + 8 - (row - top), side + 8)
        for layer in range(layers):
            for which in range(2):
                wide = tall[layer, which, pl.ds(top, side + 8), pl.ds(base, 2 * side)]
                narrow = pltpu.roll(wide, shift, 1)[:, :side]
                out_ref[w, layer, which] = pltpu.roll(narrow, lift, 0)[:side]
        return carried

    lax.fori_loop(0, rows_ref.shape[0], one, 0)


def place_kernel(rows_ref, cols_ref, pieces_ref, own_phase, own_absorb, spill_ref, tall):
    _, layers, _, side, _ = pieces_ref.shape
    cols = own_phase.shape[2]
    tall[...] = jnp.zeros_like(tall)

    def one(w, carried):
        row, col = rows_ref[w], cols_ref[w]
        base = column_base(col, side, cols)
        shift = col - base
        top = pl.multiple_of(row // 8 * 8, 8)
        for layer in range(layers):
            for which in range(2):
                piece = pieces_ref[w, layer, which]
                long = pltpu.roll(jnp.concatenate([piece, jnp.zeros_like(piece[:8])], axis=0), row - top, 0)
                wide = pltpu.roll(jnp.concatenate([long, jnp.zeros_like(long)], axis=1), shift, 1)
                where = (layer, which, pl.ds(top, side + 8), pl.ds(base, 2 * side))
                tall[where] = tall[where] + wide
        return carried

    lax.fori_loop(0, rows_ref.shape[0], one, 0)
    for layer in range(layers):
        own_phase[layer] = tall[layer, 0, :side]
        own_absorb[layer] = tall[layer, 1, :side]
        for which in range(2):
            spill_ref[which, layer] = tall[layer, which, side:]


def wave_kernel(
    place_ref, live_ref, patches, probe_ref, measured_ref,
    q_left, q_right, qa_left, qa_right, f_left, f_right, fa_left, fa_right,
    grads, trans, mixed,
):
    slabs, _, layers, _, side, _ = patches.shape
    total = slabs * layers

    def prepare(s, carried):
        slab, layer = s // layers, lax.rem(s, layers)
        damping = jnp.exp(-patches[slab, 0, layer, 1])
        cos_part, sin_part = cos_sin(patches[slab, 0, layer, 0])
        trans[s, 0] = damping * cos_part
        trans[s, 1] = damping * sin_part
        return carried

    lax.fori_loop(0, total, prepare, 0)

    def forward(s, wave):
        wave_real, wave_imag = wave
        t_real, t_imag = trans[s, 0], trans[s, 1]
        mixed_real = t_real * wave_real - t_imag * wave_imag
        mixed_imag = t_real * wave_imag + t_imag * wave_real
        mixed[s, 0] = mixed_real
        mixed[s, 1] = mixed_imag
        return sandwich(q_left, q_right, mixed_real, mixed_imag)

    wave = lax.fori_loop(0, total, forward, (probe_ref[0], probe_ref[1]))
    far_real, far_imag = sandwich(f_left, f_right, *wave)
    slot = place_ref[0] * pl.num_programs(0) + pl.program_id(0)
    held = place_ref[1]
    weight = jnp.where(slot < held, live_ref[jnp.minimum(slot, held - 1)], 0).astype(jnp.float32)
    excess = (0.5 * weight) * (far_real * far_real + far_imag * far_imag - measured_ref[0])
    back = sandwich(fa_left, fa_right, excess * far_real, excess * far_imag)

    def backward(i, back):
        s = total - 1 - i
        slab, layer = s // layers, lax.rem(s, layers)
        m_real, m_imag = sandwich(qa_left, qa_right, *back)
        u_real, u_imag = mixed[s, 0], mixed[s, 1]
        t_real, t_imag = trans[s, 0], trans[s, 1]
        grads[slab, 0, layer, 0] = u_real * m_imag - u_imag * m_real
        grads[slab, 0, layer, 1] = -(u_real * m_real + u_imag * m_imag)
        return t_real * m_real + t_imag * m_imag, t_real * m_imag - t_imag * m_real

    lax.fori_loop(0, total, backward, back)


def passed_along(array, axis, by):
    devices = lax.axis_size(axis)
    pairs = [(i, i + by) for i in range(devices) if 0 <= i + by < devices]
    return lax.ppermute(array, axis, pairs)


def params():
    return pltpu.CompilerParams(vmem_limit_bytes=vmem_limit)


def local(phase_map, absorption, probe_wave, measured, rows_at, cols_at, live_mask):
    layers, rows, cols = phase_map.shape
    side = probe_wave.shape[2]
    windows = measured.shape[0]
    slabs = lax.axis_size("slab")
    per_slab = -(-windows // slabs)
    slots = per_slab * slabs
    smem = pl.BlockSpec(memory_space=pltpu.SMEM)
    vmem = pl.BlockSpec(memory_space=pltpu.VMEM)
    f32 = jnp.float32

    below_phase, below_absorb = passed_along((phase_map, absorption), "tile", -1)
    patches = pl.pallas_call(
        cut_kernel,
        out_shape=jax.ShapeDtypeStruct((slots, layers, 2, side, side), f32),
        in_specs=[smem, smem, vmem, vmem, vmem, vmem],
        out_specs=vmem,
        scratch_shapes=[pltpu.VMEM((layers, 2, 2 * side, cols), f32)],
        compiler_params=params(),
        name="cut",
    )(rows_at, cols_at, phase_map, absorption, below_phase, below_absorb)
    patches = patches.reshape(slabs, per_slab, layers, 2, side, side)
    patches = lax.all_to_all(patches, "slab", 0, 0, tiled=True)

    place = jnp.stack([lax.axis_index("slab"), jnp.int32(windows)]).astype(jnp.int32)
    mats = [jnp.asarray(m) for m in tables(side)]
    block = (slabs, 1, layers, 2, side, side)
    whole = lambda m: pl.BlockSpec(m.shape, lambda g, *_: (0,) * m.ndim)
    grads = pl.pallas_call(
        wave_kernel,
        out_shape=jax.ShapeDtypeStruct(patches.shape, f32),
        grid_spec=pltpu.PrefetchScalarGridSpec(
            num_scalar_prefetch=2,
            grid=(per_slab,),
            in_specs=[
                pl.BlockSpec(block, lambda g, *_: (0, g, 0, 0, 0, 0)),
                whole(probe_wave),
                pl.BlockSpec(
                    (1, side, side),
                    lambda g, place, live: (jnp.minimum(place[0] * per_slab + g, windows - 1), 0, 0),
                ),
            ] + [whole(m) for m in mats],
            out_specs=pl.BlockSpec(block, lambda g, *_: (0, g, 0, 0, 0, 0)),
            scratch_shapes=[
                pltpu.VMEM((slabs * layers, 2, side, side), f32),
                pltpu.VMEM((slabs * layers, 2, side, side), f32),
            ],
        ),
        compiler_params=params(),
        name="waves",
    )(place, live_mask, patches, probe_wave, measured, *mats)

    grads = lax.all_to_all(grads, "slab", 0, 0, tiled=True)
    grads = grads.reshape(slots, layers, 2, side, side)
    own_phase, own_absorb, spill = pl.pallas_call(
        place_kernel,
        out_shape=(
            jax.ShapeDtypeStruct(phase_map.shape, f32),
            jax.ShapeDtypeStruct(phase_map.shape, f32),
            jax.ShapeDtypeStruct((2,) + phase_map.shape, f32),
        ),
        in_specs=[smem, smem, vmem],
        out_specs=(vmem, vmem, vmem),
        scratch_shapes=[pltpu.VMEM((layers, 2, 2 * side, cols), f32)],
        compiler_params=params(),
        name="place",
    )(rows_at, cols_at, grads)
    from_above = passed_along(spill, "tile", 1)
    return own_phase + from_above[0], own_absorb + from_above[1]


def solution(mesh):
    return jax.shard_map(
        local,
        mesh=mesh,
        in_specs=(
            P(("groups", "slab"), "tile", None),
            P(("groups", "slab"), "tile", None),
            P(),
            P(("groups", "tile"), None, None),
            P(("groups", "tile")),
            P(("groups", "tile")),
            P(("groups", "tile")),
        ),
        out_specs=(P(("groups", "slab"), "tile", None), P(("groups", "slab"), "tile", None)),
        check_vma=False,
    )
```

time: 637 us -> 200 us (0.31)
  local copies, waits for them, and re-layouts: 315 us -> 2.29 us
  other arithmetic: 173 us -> 3.92 us
  waiting for transfers between devices: 41 us -> 114 us
  matrix products: 47.7 us -> 0 us
  Pallas kernels: 0 us -> 35.2 us
  blocking collectives: 0 us -> 30.1 us
  starting transfers between devices: 34.5 us -> 11.4 us
  loops' own time: 17.3 us -> 0 us
    gather x8 -> x0, local copies, waits for them, and re-layouts: 211 us -> none  [the longest x1 97.2 us: tables(): kernel_real[lagged]]
    ppermute x18 -> x3, waiting for transfers between devices: 41 us -> 91.2 us  [passed_along(): return lax.ppermute(array, axis, pairs)]
    dot_general x116 -> x0, matrix products: 47.7 us -> none  [the longest x58 23.9 us: sandwich(): result = jnp.einsum('bij,jk->bik', beside, right_block, precision=highest)]
    scatter x17 -> x0, other arithmetic: 41.5 us -> none
    dynamic_update_slice x23 -> x0, local copies, waits for them, and re-layouts: 36.6 us -> none  [the longest x16 28.7 us: deposit(): lax.dynamic_update_slice(target, before + portion[slot_index], corner)]
    pallas_call x0 -> x3, Pallas kernels: none -> 35.2 us  [the longest x1 24.8 us: local(): pl.pallas_call(wave_kernel, out_shape=jax.ShapeDtypeStruct(patches.shape,...]
    sub x28 -> x0, other arithmetic: 34.3 us -> none  [forward_turn(): local_real[:, layer_index] * wave_real]
    all_to_all x0 -> x1, blocking collectives: none -> 30.1 us  [local(): grads = lax.all_to_all(grads, 'slab', 0, 0, tiled=True)]
  transfers between devices with their start and end apart: 18 -> 4, of which waited for: 8 -> 4; matrix products, arithmetic and copies ran while one was open for 43% -> 0% of each run, Pallas kernels for 0% -> 0%
where the time goes in v1:
time: 200 us; the launch traced here: 198 us
  waiting for transfers between devices  114 us (57%)
  Pallas kernels  35.2 us (18%)
  blocking collectives  30.1 us (15%)
  starting transfers between devices  11.4 us (6%)
  other arithmetic  3.92 us (2%)
  local copies, waits for them, and re-layouts  2.29 us (1%)
    ppermute x3, waiting for transfers between devices, passed_along(): return lax.ppermute(array, axis, pairs)  91.2 us
    all_to_all x1, blocking collectives, local(): grads = lax.all_to_all(grads, 'slab', 0, 0, tiled=True)  30.1 us
    pallas_call x1, Pallas kernels, local(): pl.pallas_call(wave_kernel, out_shape=jax.ShapeDtypeStruct(patches.shape,...  24.8 us
    all_to_all x1, waiting for transfers between devices, local(): patches = lax.all_to_all(patches, 'slab', 0, 0, tiled=True)  23.2 us
    ppermute x3, starting transfers between devices, passed_along(): return lax.ppermute(array, axis, pairs)  6.06 us
    pallas_call x1, Pallas kernels, local(): pl.pallas_call(cut_kernel, out_shape=jax.ShapeDtypeStruct((slots, layers,...  5.31 us
    all_to_all x1, starting transfers between devices, local(): patches = lax.all_to_all(patches, 'slab', 0, 0, tiled=True)  5.3 us
    pallas_call x1, Pallas kernels, local(): pl.pallas_call(place_kernel, out_shape=(jax.ShapeDtypeStruct(phase_map.sh...  5.11 us
  transfers between devices with their start and end apart: 4, of which 4 were waited for; matrix products, arithmetic and copies ran while one was open for 0% of the time, Pallas kernels for 0%

profile of v1, /device:TPU:19, one launch (start us, length us, event | category | flops | bytes accessed | tf_op | source)
XLA Modules:
  0.0 197.9 jit_solution(8140482458464523078)
XLA Ops:
  0.6 2.1 %collective-permute-start = (f32[4,128,512]{2,1,0:T(8,128)}, f32[4,128,512]{2,1,0:T(8,128)S(1)}, u32[]{:S(2)}, u32[]{:S(2)}) collective-permute-start(f32[4,128,512]{2,1,0:T(8,128)} %phase_ref.1), channel_id=1, source_target_pairs={{4,0},{8,4},{12,8},{5,1},{9,5},{13,9},{6,2},{10,6},{14,10},{7,3},{... | collective-permute-start | bytes 3145736 | tf_op jit(solution)/shard_map/ppermute | solution.py:195
  2.7 2.1 %collective-permute-start.1 = (f32[4,128,512]{2,1,0:T(8,128)}, f32[4,128,512]{2,1,0:T(8,128)S(1)}, u32[]{:S(2)}, u32[]{:S(2)}) collective-permute-start(f32[4,128,512]{2,1,0:T(8,128)} %absorb_ref.1), channel_id=1, source_target_pairs={{4,0},{8,4},{12,8},{5,1},{9,5},{13,9},{6,2},{10,6},{14,10},{7,3},{... | collective-permute-start | bytes 3145736 | tf_op jit(solution)/shard_map/ppermute | solution.py:195
  4.8 22.0 %collective-permute-done.below_phase_ref = f32[4,128,512]{2,1,0:T(8,128)S(1)} collective-permute-done((f32[4,128,512]{2,1,0:T(8,128)}, f32[4,128,512]{2,1,0:T(8,128)S(1)}, u32[]{:S(2)}, u32[]{:S(2)}) %collective-permute-start) | collective-permute-done | bytes 1048608 | tf_op jit(solution)/shard_map/ppermute | solution.py:195
  26.8 0.0 copy-start.1
  26.8 22.5 %collective-permute-done.1.below_absorb_ref = f32[4,128,512]{2,1,0:T(8,128)S(1)} collective-permute-done((f32[4,128,512]{2,1,0:T(8,128)}, f32[4,128,512]{2,1,0:T(8,128)S(1)}, u32[]{:S(2)}, u32[]{:S(2)}) %collective-permute-start.1) | collective-permute-done | bytes 1048608 | tf_op jit(solution)/shard_map/ppermute | solution.py:195
  49.2 0.0 copy-done.1
  49.2 0.0 copy-start.2
  49.2 1.0 copy-done.2
  50.2 5.3 %cut.1 = f32[4,4,2,128,128]{4,3,2,1,0:T(8,128)} custom-call(s32[4]{0:T(128)} %rows_ref.3, s32[4]{0:T(128)} %cols_ref.3, f32[4,128,512]{2,1,0:T(8,128)} %phase_ref.1, f32[4,128,512]{2,1,0:T(8,128)} %absorb_ref.1, f32[4,128,512]{2,1,0:T(8,128)} %copy-done.1, f32[4,128,512]{2,1,0:T(8,128)} %copy-done.2), custom_call_target="tpu_custom_call" | custom-call | tf_op jit(solution)/shard_map/cut/pallas_call | solution.py:214
  55.5 5.3 %all-to-all-start = ((f32[4,1,4,2,128,128]{5,4,3,2,1,0:T(8,128)}), f32[4,1,4,2,128,128]{5,4,3,2,1,0:T(8,128)S(1)}, u32[]{:S(2)}, u32[]{:S(2)}) async-start(f32[4,1,4,2,128,128]{5,4,3,2,1,0:T(8,128)} %bitcast.11), calls=%async_computation | async-start | bytes 4194304 | tf_op jit(solution)/shard_map/all_to_all | solution.py:224
  60.8 0.6 pad_add_fusion.place_ref
  61.4 23.2 %all-to-all-done.patches = f32[4,1,4,2,128,128]{5,4,3,2,1,0:T(8,128)S(1)} async-done(((f32[4,1,4,2,128,128]{5,4,3,2,1,0:T(8,128)}), f32[4,1,4,2,128,128]{5,4,3,2,1,0:T(8,128)S(1)}, u32[]{:S(2)}, u32[]{:S(2)}) %all-to-all-start) | async-done | bytes 2097184 | tf_op jit(solution)/shard_map/all_to_all | solution.py:224
  84.6 0.0 copy-start
  84.6 1.3 copy-done
  85.9 24.8 %waves.1 = f32[4,1,4,2,128,128]{5,4,3,2,1,0:T(8,128)} custom-call(s32[2]{0:T(128)} %pad_add_fusion.place_ref, s32[4]{0:T(128)} %live_ref.1, f32[4,1,4,2,128,128]{5,4,3,2,1,0:T(8,128)} %copy-done, f32[2,128,128]{2,1,0:T(8,128)} %probe_ref.1, f32[4,128,128]{2,1,0:T(8,128)} %measured_ref.1, bf16[256,768]{1,0:T(8,128)(2,1)} %constant.22.clone.q_left, ...), custom_call_target="tpu_custom_call" | custom-call | tf_op jit(solution)/shard_map/waves/pallas_call | solution.py:230
  110.7 30.1 %all_to_all.10 = f32[4,1,4,2,128,128]{5,4,3,2,1,0:T(8,128)} all-to-all(f32[4,1,4,2,128,128]{5,4,3,2,1,0:T(8,128)} %waves.1), channel_id=1, replica_groups=mesh['groups'=2,'tile'=4,'slab'=4] {'slab'}, dimensions={0} | all-to-all | bytes 4194304 | tf_op jit(solution)/shard_map/all_to_all | solution.py:254
  140.8 5.1 %place.1 = (f32[4,128,512]{2,1,0:T(8,128)}, f32[4,128,512]{2,1,0:T(8,128)}, f32[2,4,128,512]{3,2,1,0:T(8,128)}) custom-call(s32[4]{0:T(128)} %rows_ref.3, s32[4]{0:T(128)} %cols_ref.3, f32[4,4,2,128,128]{4,3,2,1,0:T(8,128)} %bitcast.12), custom_call_target="tpu_custom_call" | custom-call | tf_op jit(solution)/shard_map/place/pallas_call | solution.py:256
  145.9 1.9 collective-permute-start.2
  147.9 46.7 %collective-permute-done.2 = f32[2,4,128,512]{3,2,1,0:T(8,128)S(1)} collective-permute-done((f32[2,4,128,512]{3,2,1,0:T(8,128)}, f32[2,4,128,512]{3,2,1,0:T(8,128)S(1)}, u32[]{:S(2)}, u32[]{:S(2)}) %collective-permute-start.2) | collective-permute-done | bytes 2097184 | tf_op jit(solution)/shard_map/ppermute | solution.py:195
  194.6 3.3 %fusion = (f32[4,128,512]{2,1,0:T(8,128)}, f32[4,128,512]{2,1,0:T(8,128)}) fusion(f32[4,128,512]{2,1,0:T(8,128)} %get-tuple-element.7, f32[2,4,128,512]{3,2,1,0:T(8,128)S(1)} %collective-permute-done.2, f32[4,128,512]{2,1,0:T(8,128)} %get-tuple-element.5), kind=kLoop, calls=%fused_computation.1 | loop fusion | flops 524288 | bytes 6291456 | tf_op jit(solution)/shard_map/add | solution.py:270
Async XLA Ops:
  0.6 26.1 %collective-permute-start = (f32[4,128,512]{2,1,0:T(8,128)}, f32[4,128,512]{2,1,0:T(8,128)S(1)}, u32[]{:S(2)}, u32[]{:S(2)}) collective-permute-start(f32[4,128,512]{2,1,0:T(8,128)} %phase_ref.1), channel_id=1, source_target_pairs={{4,0},{8,4},{12,8},{5,1},{9,5},{13,9},{6,2},{10,6},{14,10},{7,3},{... | collective-permute-start | bytes 3145736 | tf_op jit(solution)/shard_map/ppermute | solution.py:195
  2.7 46.5 %collective-permute-start.1 = (f32[4,128,512]{2,1,0:T(8,128)}, f32[4,128,512]{2,1,0:T(8,128)S(1)}, u32[]{:S(2)}, u32[]{:S(2)}) collective-permute-start(f32[4,128,512]{2,1,0:T(8,128)} %absorb_ref.1), channel_id=1, source_target_pairs={{4,0},{8,4},{12,8},{5,1},{9,5},{13,9},{6,2},{10,6},{14,10},{7,3},{... | collective-permute-start | bytes 3145736 | tf_op jit(solution)/shard_map/ppermute | solution.py:195
  26.8 22.5 %copy-start.1 = (f32[4,128,512]{2,1,0:T(8,128)}, f32[4,128,512]{2,1,0:T(8,128)S(1)}, u32[]{:S(2)}) copy-start(f32[4,128,512]{2,1,0:T(8,128)S(1)} %collective-permute-done.below_phase_ref) | copy-start | bytes 3145732
  49.2 1.0 copy-start.2
  55.5 29.1 %all-to-all-start = ((f32[4,1,4,2,128,128]{5,4,3,2,1,0:T(8,128)}), f32[4,1,4,2,128,128]{5,4,3,2,1,0:T(8,128)S(1)}, u32[]{:S(2)}, u32[]{:S(2)}) async-start(f32[4,1,4,2,128,128]{5,4,3,2,1,0:T(8,128)} %bitcast.11), calls=%async_computation | async-start | bytes 4194304 | tf_op jit(solution)/shard_map/all_to_all | solution.py:224
  84.6 1.3 copy-start
  145.9 48.7 %collective-permute-start.2 = (f32[2,4,128,512]{3,2,1,0:T(8,128)}, f32[2,4,128,512]{3,2,1,0:T(8,128)S(1)}, u32[]{:S(2)}, u32[]{:S(2)}) collective-permute-start(f32[2,4,128,512]{3,2,1,0:T(8,128)} %get-tuple-element.6), channel_id=1, source_target_pairs={{0,4},{4,8},{8,12},{1,5},{5,9},{9,13},{2,6},{6,10},{10,14},{3,7},{... | collective-permute-start | bytes 6291464 | tf_op jit(solution)/shard_map/ppermute | solution.py:195

commit v2 on v1

v2 whole, which is shorter than its diff:
```python
import functools
import math

import jax
import jax.numpy as jnp
import ml_dtypes
import numpy as np
from jax import lax
from jax.experimental import pallas as pl
from jax.experimental.pallas import tpu as pltpu
from jax.sharding import PartitionSpec as P

chirp_rate = 0.25
MESH = pl.DeviceIdType.MESH
vmem_limit = 56 * 1024 * 1024


def split_host(mat):
    high = mat.astype(np.float32).astype(ml_dtypes.bfloat16)
    low = (mat - high.astype(np.float64)).astype(np.float32).astype(ml_dtypes.bfloat16)
    return high, low


def tables(length):
    index = np.arange(length)
    signed = np.where(index < length // 2, index, index - length).astype(np.float64)
    chirped = -np.pi * chirp_rate * signed * signed / length
    rotation = 2.0 * np.pi * (index[:, None] * index[None, :] % length) / length
    kernel = np.exp(1j * (chirped[:, None] + rotation)).sum(axis=0) / length
    spread = kernel[(index[:, None] - index[None, :]) % length]
    fourier = np.exp(-1j * rotation) / math.sqrt(length)
    forms = []
    for mat in (spread, fourier):
        re, im = mat.real, mat.imag
        minus = np.block([[re, im], [-im, re]])
        plus = np.block([[re, -im], [im, re]])
        for block in (minus, plus):
            high, low = split_host(block)
            forms.append(
                (np.concatenate([high, high, low], axis=0), np.concatenate([high, high, low], axis=1))
            )
    (q_minus, q_plus, f_minus, f_plus) = forms
    return (
        q_plus[1], q_minus[0], q_minus[1], q_plus[0],
        f_plus[1], f_minus[0], f_minus[1], f_plus[0],
    )


def halves(array):
    high = array.astype(jnp.bfloat16)
    low = (array - high.astype(jnp.float32)).astype(jnp.bfloat16)
    return high, low


def sandwich(left_ref, right_ref, wave_real, wave_imag):
    side = wave_real.shape[0]
    high, low = halves(jnp.concatenate([wave_real, wave_imag], axis=1))
    beside = jnp.dot(
        jnp.concatenate([high, low, high], axis=1), right_ref[...],
        preferred_element_type=jnp.float32,
    )
    high, low = halves(jnp.concatenate([beside[:, :side], beside[:, side:]], axis=0))
    stacked = jnp.dot(
        left_ref[...], jnp.concatenate([high, low, high], axis=0),
        preferred_element_type=jnp.float32,
    )
    return stacked[:side], stacked[side:]


def cos_sin(angle):
    turns = jnp.floor(angle * (2.0 / math.pi) + 0.5)
    rest = angle - turns * 1.5703125
    rest = rest - turns * 4.837512969970703e-4
    rest = rest - turns * 7.549789948768648e-8
    sq = rest * rest
    sin_part = rest + rest * sq * (-1.6666654611e-1 + sq * (8.3321608736e-3 + sq * -1.9515295891e-4))
    cos_part = 1.0 - 0.5 * sq + sq * sq * (
        4.166664568298827e-2 + sq * (-1.388731625493765e-3 + sq * 2.443315711809948e-5)
    )
    half = jnp.floor(turns * 0.5)
    odd = (turns - 2.0 * half) > 0.5
    flip = 1.0 - 2.0 * (half - 2.0 * jnp.floor(half * 0.5))
    cos_out = jnp.where(odd, -sin_part, cos_part) * flip
    sin_out = jnp.where(odd, cos_part, sin_part) * flip
    return cos_out, sin_out


def column_base(col, side, cols):
    return pl.multiple_of(jnp.minimum(col // side, cols // side - 2) * side, side)


def cut_kernel(own_ref, above_ref, phase_ref, absorb_ref, own_out, above_out, tall):
    windows, layers, _, side, _ = own_out.shape
    cols = phase_ref.shape[2]
    for layer in range(layers):
        for which, source in enumerate((phase_ref, absorb_ref)):
            blank = jnp.zeros((side, cols), jnp.float32)
            tall[layer, which, :side] = blank
            tall[layer, which, side : 2 * side] = source[layer]
            tall[layer, which, 2 * side :] = blank

    def one(w, carried):
        for index_ref, out_ref, start in ((own_ref, own_out, side), (above_ref, above_out, 0)):
            row, col = index_ref[w], index_ref[windows + w]
            base = column_base(col, side, cols)
            shift = lax.rem(2 * side - (col - base), 2 * side)
            top = pl.multiple_of(row // 8 * 8, 8)
            lift = lax.rem(side + 8 - (row - top), side + 8)
            for layer in range(layers):
                for which in range(2):
                    wide = tall[layer, which, pl.ds(start + top, side + 8), pl.ds(base, 2 * side)]
                    narrow = pltpu.roll(wide, shift, 1)[:, :side]
                    out_ref[w, layer, which] = pltpu.roll(narrow, lift, 0)[:side]
        return carried

    lax.fori_loop(0, windows, one, 0)


def place_kernel(own_ref, above_ref, own_pieces, above_pieces, out_phase, out_absorb, tall):
    windows, layers, _, side, _ = own_pieces.shape
    cols = out_phase.shape[2]
    tall[...] = jnp.zeros_like(tall)

    def place(index_ref, pieces_ref, start, w):
        row, col = index_ref[w], index_ref[windows + w]
        base = column_base(col, side, cols)
        shift = col - base
        top = pl.multiple_of(row // 8 * 8, 8)
        for layer in range(layers):
            for which in range(2):
                piece = pieces_ref[w, layer, which]
                long = pltpu.roll(jnp.concatenate([piece, jnp.zeros_like(piece[:8])], axis=0), row - top, 0)
                wide = pltpu.roll(jnp.concatenate([long, jnp.zeros_like(long)], axis=1), shift, 1)
                where = (layer, which, pl.ds(start + top, side + 8), pl.ds(base, 2 * side))
                tall[where] = tall[where] + wide

    @pl.loop(0, windows)
    def _(w):
        place(own_ref, own_pieces, side, w)

        @pl.when(lax.axis_index("tile") > 0)
        def _():
            place(above_ref, above_pieces, 0, w)

    for layer in range(layers):
        out_phase[layer] = tall[layer, 0, side : 2 * side]
        out_absorb[layer] = tall[layer, 1, side : 2 * side]


def greet():
    slab, slabs = lax.axis_index("slab"), lax.axis_size("slab")
    tile, tiles = lax.axis_index("tile"), lax.axis_size("tile")
    barrier = pltpu.get_barrier_semaphore()
    for step in range(1, slabs):
        pl.semaphore_signal(
            barrier, inc=1, device_id={"slab": lax.rem(slab + step, slabs)}, device_id_type=MESH
        )

    @pl.when(tile > 0)
    def _():
        pl.semaphore_signal(barrier, inc=1, device_id={"tile": tile - 1}, device_id_type=MESH)

    @pl.when(tile < tiles - 1)
    def _():
        pl.semaphore_signal(barrier, inc=1, device_id={"tile": tile + 1}, device_id_type=MESH)

    beside = (tile > 0).astype(jnp.int32) + (tile < tiles - 1).astype(jnp.int32)
    pl.semaphore_wait(barrier, slabs - 1 + beside)


def slot_plan(windows, slabs):
    moved = windows // 2
    kept = windows - moved
    return kept, moved, -(-(windows + moved) // slabs)


def gather_kernel(own, above, patches, from_below, from_above, merged, zs_sem, zr_sem, xs_sem, xr_sem):
    windows, layers = own.shape[:2]
    slab, slabs = lax.axis_index("slab"), lax.axis_size("slab")
    tile, tiles = lax.axis_index("tile"), lax.axis_size("tile")
    kept, moved, _ = slot_plan(windows, slabs)
    first, last = tile == 0, tile == tiles - 1
    greet()

    def up(i, l):
        return pltpu.make_async_remote_copy(
            src_ref=above.at[i, l], dst_ref=from_below.at[i, l], send_sem=zs_sem.at[i, l],
            recv_sem=zr_sem.at[i, l], device_id={"tile": tile - 1}, device_id_type=MESH)

    def down(j, l):
        return pltpu.make_async_remote_copy(
            src_ref=own.at[kept + j, l], dst_ref=from_above.at[j, l], send_sem=zs_sem.at[kept + j, l],
            recv_sem=zr_sem.at[kept + j, l], device_id={"tile": tile + 1}, device_id_type=MESH)

    def across(k, source, l, sender):
        return pltpu.make_async_remote_copy(
            src_ref=source, dst_ref=patches.at[k // slabs, sender * layers + l], send_sem=xs_sem.at[k, l],
            recv_sem=xr_sem.at[k // slabs, sender, l], device_id={"slab": k % slabs}, device_id_type=MESH)

    @pl.loop(0, layers)
    def _(l):
        @pl.when(jnp.logical_not(first))
        def _():
            for i in range(kept):
                up(i, l).start()

        @pl.when(jnp.logical_not(last))
        def _():
            for j in range(moved):
                down(j, l).start()

    def hand_over(k, source, l):
        @pl.when(slab != k % slabs)
        def _():
            across(k, source, l, slab).start()

        @pl.when(slab == k % slabs)
        def _():
            patches[k // slabs, slab * layers + l] = source[...]

    @pl.when(last)
    def _():
        @pl.loop(0, layers)
        def _(l):
            for j in range(moved):
                hand_over(windows + j, own.at[kept + j, l], l)

    @pl.loop(0, layers)
    def _(l):
        for i in range(kept):
            @pl.when(last)
            def _():
                merged[i, l] = own[i, l]

            @pl.when(jnp.logical_not(last))
            def _():
                up(i, l).wait_recv()
                merged[i, l] = own[i, l] + from_below[i, l]

            hand_over(i, merged.at[i, l], l)

        @pl.when(jnp.logical_not(first))
        def _():
            for j in range(moved):
                down(j, l).wait_recv()
                merged[kept + j, l] = above[kept + j, l] + from_above[j, l]
                hand_over(kept + j, merged.at[kept + j, l], l)

    def finish(k, source):
        @pl.when(slab != k % slabs)
        def _():
            @pl.loop(0, layers)
            def _(l):
                across(k, source.at[l], l, slab).wait_send()

        @pl.when(slab == k % slabs)
        def _():
            for sender in range(slabs):
                @pl.when(sender != slab)
                def _():
                    @pl.loop(0, layers)
                    def _(l):
                        across(k, source.at[l], l, sender).wait_recv()

    for i in range(kept):
        finish(i, merged.at[i])

    @pl.when(jnp.logical_not(first))
    def _():
        for j in range(moved):
            finish(kept + j, merged.at[kept + j])

        @pl.loop(0, layers)
        def _(l):
            for i in range(kept):
                up(i, l).wait_send()

    @pl.when(last)
    def _():
        for j in range(moved):
            finish(windows + j, own.at[kept + j])

    @pl.when(jnp.logical_not(last))
    def _():
        @pl.loop(0, layers)
        def _(l):
            for j in range(moved):
                down(j, l).wait_send()


def scatter_kernel(grads, own, above, zs_sem, xs_sem, own_sem, above_sem):
    windows, layers = own.shape[:2]
    slab, slabs = lax.axis_index("slab"), lax.axis_size("slab")
    tile, tiles = lax.axis_index("tile"), lax.axis_size("tile")
    kept, moved, _ = slot_plan(windows, slabs)
    first, last = tile == 0, tile == tiles - 1
    greet()

    def home(k, l):
        if k < kept:
            return own.at[k, l], own_sem.at[k, l]
        if k < windows:
            return above.at[k, l], above_sem.at[k, l]
        return own.at[k - moved, l], own_sem.at[k - moved, l]

    def across(k, l, target):
        place, sem = home(k, l)
        return pltpu.make_async_remote_copy(
            src_ref=grads.at[k // slabs, target * layers + l], dst_ref=place,
            send_sem=xs_sem.at[k // slabs, target, l], recv_sem=sem,
            device_id={"slab": target}, device_id_type=MESH)

    def down(i, l):
        return pltpu.make_async_remote_copy(
            src_ref=own.at[i, l], dst_ref=above.at[i, l], send_sem=zs_sem.at[i, l],
            recv_sem=above_sem.at[i, l], device_id={"tile": tile + 1}, device_id_type=MESH)

    def up(k, l):
        return pltpu.make_async_remote_copy(
            src_ref=above.at[k, l], dst_ref=own.at[k, l], send_sem=zs_sem.at[k, l],
            recv_sem=own_sem.at[k, l], device_id={"tile": tile - 1}, device_id_type=MESH)

    def give(k, l):
        @pl.when(slab == k % slabs)
        def _():
            for target in range(slabs):
                @pl.when(slab != target)
                def _():
                    across(k, l, target).start()

            home(k, l)[0][...] = grads[k // slabs, slab * layers + l]

    @pl.loop(0, layers)
    def _(l):
        for k in range(kept):
            give(k, l)

        @pl.when(jnp.logical_not(first))
        def _():
            for k in range(kept, windows):
                give(k, l)

        @pl.when(last)
        def _():
            for k in range(windows, windows + moved):
                give(k, l)

    def arrive(k, l):
        @pl.when(slab != k % slabs)
        def _():
            across(k, l, slab).wait_recv()

    @pl.loop(0, layers)
    def _(l):
        for k in range(kept):
            arrive(k, l)

            @pl.when(jnp.logical_not(last))
            def _():
                down(k, l).start()

        @pl.when(jnp.logical_not(first))
        def _():
            for k in range(kept, windows):
                arrive(k, l)
                up(k, l).start()

    def sent(k, l):
        @pl.when(slab == k % slabs)
        def _():
            for target in range(slabs):
                @pl.when(slab != target)
                def _():
                    across(k, l, target).wait_send()

    @pl.loop(0, layers)
    def _(l):
        for k in range(kept):
            sent(k, l)

        @pl.when(jnp.logical_not(first))
        def _():
            for k in range(kept, windows):
                sent(k, l)
                up(k, l).wait_send()
            for k in range(kept):
                down(k, l).wait_recv()

        @pl.when(jnp.logical_not(last))
        def _():
            for k in range(kept):
                down(k, l).wait_send()
            for k in range(kept, windows):
                up(k, l).wait_recv()

        @pl.when(last)
        def _():
            for k in range(windows, windows + moved):
                arrive(k, l)
                sent(k, l)


def wave_kernel(
    own_ref, above_ref, patches, probe_ref, measured_ref, above_measured_ref,
    q_left, q_right, qa_left, qa_right, f_left, f_right, fa_left, fa_right,
    grads, trans, mixed,
):
    depth, total, _, side, _ = patches.shape
    windows = measured_ref.shape[0]
    slab, slabs = lax.axis_index("slab"), lax.axis_size("slab")
    tile, tiles = lax.axis_index("tile"), lax.axis_size("tile")
    kept, moved, _ = slot_plan(windows, slabs)

    def valid(d):
        k = d * slabs + slab
        mine = k < kept
        from_above = (k >= kept) & (k < windows) & (tile > 0)
        extra = (k >= windows) & (k < windows + moved) & (tile == tiles - 1)
        return mine | from_above | extra

    def far_side(d, wave):
        k = d * slabs + slab
        is_above = (k >= kept) & (k < windows)
        own_at = jnp.clip(jnp.where(k < windows, k, k - moved), 0, windows - 1)
        above_at = jnp.clip(k, kept, windows - 1)
        live = jnp.where(is_above, above_ref[2 * windows + above_at], own_ref[2 * windows + own_at])
        target = jnp.where(is_above, above_measured_ref[above_at - kept], measured_ref[own_at])
        far_real, far_imag = sandwich(f_left, f_right, *wave)
        excess = (0.5 * live.astype(jnp.float32)) * (far_real * far_real + far_imag * far_imag - target)
        return sandwich(fa_left, fa_right, excess * far_real, excess * far_imag)

    def run(slots):
        def prepare(s, carried):
            for d in slots:
                damping = jnp.exp(-patches[d, s, 1])
                cos_part, sin_part = cos_sin(patches[d, s, 0])
                trans[d, s, 0] = damping * cos_part
                trans[d, s, 1] = damping * sin_part
            return carried

        lax.fori_loop(0, total, prepare, 0)

        def forward(s, waves):
            entering = []
            for d, (wave_real, wave_imag) in zip(slots, waves):
                t_real, t_imag = trans[d, s, 0], trans[d, s, 1]
                mixed_real = t_real * wave_real - t_imag * wave_imag
                mixed_imag = t_real * wave_imag + t_imag * wave_real
                mixed[d, s, 0] = mixed_real
                mixed[d, s, 1] = mixed_imag
                entering.append((mixed_real, mixed_imag))
            return tuple(sandwich(q_left, q_right, *wave) for wave in entering)

        waves = lax.fori_loop(0, total, forward, tuple((probe_ref[0], probe_ref[1]) for d in slots))
        backs = tuple(far_side(d, wave) for d, wave in zip(slots, waves))

        def backward(i, backs):
            s = total - 1 - i
            result = []
            for d, (m_real, m_imag) in zip(slots, [sandwich(qa_left, qa_right, *back) for back in backs]):
                u_real, u_imag = mixed[d, s, 0], mixed[d, s, 1]
                t_real, t_imag = trans[d, s, 0], trans[d, s, 1]
                grads[d, s, 0] = u_real * m_imag - u_imag * m_real
                grads[d, s, 1] = -(u_real * m_real + u_imag * m_imag)
                result.append((t_real * m_real + t_imag * m_imag, t_real * m_imag - t_imag * m_real))
            return tuple(result)

        lax.fori_loop(0, total, backward, backs)

    deeper = valid(1) if depth > 1 else jnp.bool_(False)

    @pl.when(valid(0) & jnp.logical_not(deeper))
    def _():
        run([0])

    if depth > 1:
        @pl.when(deeper)
        def _():
            run(list(range(depth)))


def passed_along(array, axis, by):
    devices = lax.axis_size(axis)
    pairs = [(i, i + by) for i in range(devices) if 0 <= i + by < devices]
    return lax.ppermute(array, axis, pairs)


def params(**more):
    return pltpu.CompilerParams(vmem_limit_bytes=vmem_limit, **more)


def local(phase_map, absorption, probe_wave, measured, rows_at, cols_at, live_mask):
    layers, rows, cols = phase_map.shape
    side = probe_wave.shape[2]
    windows = measured.shape[0]
    slabs = lax.axis_size("slab")
    kept, moved, depth = slot_plan(windows, slabs)
    smem = pl.BlockSpec(memory_space=pltpu.SMEM)
    vmem = pl.BlockSpec(memory_space=pltpu.VMEM)
    f32 = jnp.float32
    dma = pltpu.SemaphoreType.DMA
    pieces = jax.ShapeDtypeStruct((windows, layers, 2, side, side), f32)
    stacked = jax.ShapeDtypeStruct((depth, slabs * layers, 2, side, side), f32)

    index_own = jnp.concatenate([rows_at, cols_at, live_mask])
    index_above = passed_along(index_own, "tile", 1)
    measured_above = passed_along(measured[kept:], "tile", 1)
    own, above = pl.pallas_call(
        cut_kernel,
        out_shape=(pieces, pieces),
        in_specs=[smem, smem, vmem, vmem],
        out_specs=(vmem, vmem),
        scratch_shapes=[pltpu.VMEM((layers, 2, 3 * side, cols), f32)],
        compiler_params=params(),
        name="cut",
    )(index_own, index_above, phase_map, absorption)
    patches = pl.pallas_call(
        gather_kernel,
        out_shape=stacked,
        in_specs=[vmem, vmem],
        out_specs=vmem,
        scratch_shapes=[
            pltpu.VMEM((kept,) + pieces.shape[1:], f32),
            pltpu.VMEM((moved,) + pieces.shape[1:], f32),
            pltpu.VMEM(pieces.shape, f32),
            dma((windows, layers)),
            dma((windows, layers)),
            dma((windows + moved, layers)),
            dma((depth, slabs, layers)),
        ],
        compiler_params=params(collective_id=0, has_side_effects=True),
        name="gather",
    )(own, above)

    mats = [jnp.asarray(m) for m in tables(side)]
    grads = pl.pallas_call(
        wave_kernel,
        out_shape=stacked,
        in_specs=[smem, smem] + [vmem] * (4 + len(mats)),
        out_specs=vmem,
        scratch_shapes=[pltpu.VMEM(stacked.shape, f32), pltpu.VMEM(stacked.shape, f32)],
        compiler_params=params(),
        name="waves",
    )(index_own, index_above, patches, probe_wave, measured, measured_above, *mats)

    own, above = pl.pallas_call(
        scatter_kernel,
        out_shape=(pieces, pieces),
        in_specs=[vmem],
        out_specs=(vmem, vmem),
        scratch_shapes=[
            dma((windows, layers)),
            dma((depth, slabs, layers)),
            dma((windows, layers)),
            dma((windows, layers)),
        ],
        compiler_params=params(collective_id=1, has_side_effects=True),
        name="scatter",
    )(grads)
    whole = jax.ShapeDtypeStruct(phase_map.shape, f32)
    return pl.pallas_call(
        place_kernel,
        out_shape=(whole, whole),
        in_specs=[smem, smem, vmem, vmem],
        out_specs=(vmem, vmem),
        scratch_shapes=[pltpu.VMEM((layers, 2, 3 * side, cols), f32)],
        compiler_params=params(),
        name="place",
    )(index_own, index_above, own, above)


def solution(mesh):
    return jax.shard_map(
        local,
        mesh=mesh,
        in_specs=(
            P(("groups", "slab"), "tile", None),
            P(("groups", "slab"), "tile", None),
            P(),
            P(("groups", "tile"), None, None),
            P(("groups", "tile")),
            P(("groups", "tile")),
            P(("groups", "tile")),
        ),
        out_specs=(P(("groups", "slab"), "tile", None), P(("groups", "slab"), "tile", None)),
        check_vma=False,
    )
```

time: 200 us -> 168 us (0.84)
  Pallas kernels: 35.2 us -> 156 us
  waiting for transfers between devices: 114 us -> 2.36 us
  blocking collectives: 30.1 us -> 0 us
  starting transfers between devices: 11.4 us -> 5.11 us
  other arithmetic: 3.92 us -> 0.77 us
    pallas_call x3 -> x5, Pallas kernels: 35.2 us -> 156 us  [the longest x1 80.9 us: local(): pl.pallas_call(scatter_kernel, out_shape=(pieces, pieces), in_specs=[vmem...]
    ppermute x3 -> x2, waiting for transfers between devices: 91.2 us -> 2.36 us  [passed_along(): return lax.ppermute(array, axis, pairs)]
    all_to_all x1 -> x0, blocking collectives: 30.1 us -> none  [local(): grads = lax.all_to_all(grads, 'slab', 0, 0, tiled=True)]
    all_to_all x1 -> x0, waiting for transfers between devices: 23.2 us -> none  [local(): patches = lax.all_to_all(patches, 'slab', 0, 0, tiled=True)]
    all_to_all x1 -> x0, starting transfers between devices: 5.3 us -> none  [local(): patches = lax.all_to_all(patches, 'slab', 0, 0, tiled=True)]
    add x1 -> x0, other arithmetic: 3.33 us -> none  [local(): return (own_phase + from_above[0], own_absorb + from_above[1])]
    ppermute x3 -> x2, starting transfers between devices: 6.06 us -> 5.11 us  [passed_along(): return lax.ppermute(array, axis, pairs)]
  transfers between devices with their start and end apart: 4 -> 2, of which waited for: 4 -> 1; matrix products, arithmetic and copies ran while one was open for 0% -> 0% of each run, Pallas kernels for 0% -> 26%
where the time goes in v2:
time: 168 us; the launch traced here: 167 us
  Pallas kernels  156 us (93%)
  starting transfers between devices  5.11 us (3%)
  waiting for transfers between devices  2.36 us (1%)
  local copies, waits for them, and re-layouts  2.14 us (1%)
    pallas_call x1, Pallas kernels, local(): pl.pallas_call(scatter_kernel, out_shape=(pieces, pieces), in_specs=[vmem...  80.9 us
    pallas_call x1, Pallas kernels, local(): pl.pallas_call(gather_kernel, out_shape=stacked, in_specs=[vmem, vmem], o...  37.5 us
    pallas_call x1, Pallas kernels, local(): pl.pallas_call(wave_kernel, out_shape=stacked, in_specs=[smem, smem] + [v...  25.3 us
    pallas_call x1, Pallas kernels, local(): pl.pallas_call(place_kernel, out_shape=(whole, whole), in_specs=[smem, sm...  6.38 us
    pallas_call x1, Pallas kernels, local(): pl.pallas_call(cut_kernel, out_shape=(pieces, pieces), in_specs=[smem, sm...  6.31 us
    ppermute x2, starting transfers between devices, passed_along(): return lax.ppermute(array, axis, pairs)  5.11 us
  transfers between devices with their start and end apart: 2, of which 1 were waited for; matrix products, arithmetic and copies ran while one was open for 0% of the time, Pallas kernels for 26%

profile of v2, /device:TPU:19, one launch (start us, length us, event | category | flops | bytes accessed | tf_op | source)
XLA Modules:
  0.0 167.5 jit_solution(13573855477691506020)
XLA Ops:
  0.6 0.9 slice.3
  1.5 3.2 %collective-permute-start.1 = (f32[2,128,128]{2,1,0:T(8,128)S(1)}, f32[2,128,128]{2,1,0:T(8,128)S(1)}, u32[]{:S(2)}, u32[]{:S(2)}) collective-permute-start(f32[2,128,128]{2,1,0:T(8,128)S(1)} %slice.3), channel_id=1, source_target_pairs={{0,4},{4,8},{8,12},{1,5},{5,9},{9,13},{2,6},{6,10},{10,14},{3,7},{... | collective-permute-start | bytes 393224 | tf_op jit(solution)/shard_map/ppermute | solution.py:485
  4.8 0.8 pad_add_fusion.own_ref
  5.5 0.0 copy-start.1
  5.5 1.9 %collective-permute-start = (s32[12]{0:T(128)S(1)}, s32[12]{0:T(128)S(1)}, u32[]{:S(2)}, u32[]{:S(2)}) collective-permute-start(s32[12]{0:T(128)S(1)} %pad_add_fusion.own_ref), channel_id=1, source_target_pairs={{0,4},{4,8},{8,12},{1,5},{5,9},{9,13},{2,6},{6,10},{10,14},{3,7},{... | collective-permute-start | bytes 152 | tf_op jit(solution)/shard_map/ppermute | solution.py:485
  7.4 2.4 %collective-permute-done.above_ref = s32[12]{0:T(128)S(1)} collective-permute-done((s32[12]{0:T(128)S(1)}, s32[12]{0:T(128)S(1)}, u32[]{:S(2)}, u32[]{:S(2)}) %collective-permute-start) | collective-permute-done | bytes 80 | tf_op jit(solution)/shard_map/ppermute | solution.py:485
  9.8 0.0 copy-done.1
  9.8 0.0 copy-start.2
  9.8 0.6 copy-done.2
  10.4 6.3 %cut.1 = (f32[4,4,2,128,128]{4,3,2,1,0:T(8,128)}, f32[4,4,2,128,128]{4,3,2,1,0:T(8,128)}) custom-call(s32[12]{0:T(128)} %copy-done.1, s32[12]{0:T(128)} %copy-done.2, f32[4,128,512]{2,1,0:T(8,128)} %phase_ref.1, f32[4,128,512]{2,1,0:T(8,128)} %absorb_ref.1), custom_call_target="tpu_custom_call" | custom-call | tf_op jit(solution)/shard_map/cut/pallas_call | solution.py:508
  16.7 37.5 %gather.1.patches = f32[2,16,2,128,128]{4,3,2,1,0:T(8,128)} custom-call(f32[4,4,2,128,128]{4,3,2,1,0:T(8,128)} %get-tuple-element.6.own, f32[4,4,2,128,128]{4,3,2,1,0:T(8,128)} %get-tuple-element.7.above), custom_call_target="tpu_custom_call" | custom-call | tf_op jit(solution)/shard_map/gather/pallas_call | solution.py:517
  54.2 0.0 collective-permute-done.1.above_measured_ref
  54.2 0.0 copy-start
  54.2 0.6 copy-done
  54.9 25.3 %waves.1.grads = f32[2,16,2,128,128]{4,3,2,1,0:T(8,128)} custom-call(s32[12]{0:T(128)} %copy-done.1, s32[12]{0:T(128)} %copy-done.2, f32[2,16,2,128,128]{4,3,2,1,0:T(8,128)} %gather.1.patches, f32[2,128,128]{2,1,0:T(8,128)} %probe_ref.1, f32[4,128,128]{2,1,0:T(8,128)} %measured_ref.1, f32[2,128,128]{2,1,0:T(8,128)} %copy-done, ...), custom_call_target="tpu_custom_call" | custom-call | tf_op jit(solution)/shard_map/waves/pallas_call | solution.py:536
  80.2 80.9 %scatter.1 = (f32[4,4,2,128,128]{4,3,2,1,0:T(8,128)}, f32[4,4,2,128,128]{4,3,2,1,0:T(8,128)}) custom-call(f32[2,16,2,128,128]{4,3,2,1,0:T(8,128)} %waves.1.grads), custom_call_target="tpu_custom_call" | custom-call | tf_op jit(solution)/shard_map/scatter/pallas_call | solution.py:546
  161.1 6.4 %place.1 = (f32[4,128,512]{2,1,0:T(8,128)}, f32[4,128,512]{2,1,0:T(8,128)}) custom-call(s32[12]{0:T(128)} %copy-done.1, s32[12]{0:T(128)} %copy-done.2, f32[4,4,2,128,128]{4,3,2,1,0:T(8,128)} %get-tuple-element.8.own_pieces, f32[4,4,2,128,128]{4,3,2,1,0:T(8,128)} %get-tuple-element.9.above_pieces), custom_call_target="tpu_custom_call" | custom-call | tf_op jit(solution)/shard_map/place/pallas_call | solution.py:561
Async XLA Ops:
  1.5 52.6 %collective-permute-start.1 = (f32[2,128,128]{2,1,0:T(8,128)S(1)}, f32[2,128,128]{2,1,0:T(8,128)S(1)}, u32[]{:S(2)}, u32[]{:S(2)}) collective-permute-start(f32[2,128,128]{2,1,0:T(8,128)S(1)} %slice.3), channel_id=1, source_target_pairs={{0,4},{4,8},{8,12},{1,5},{5,9},{9,13},{2,6},{6,10},{10,14},{3,7},{... | collective-permute-start | bytes 393224 | tf_op jit(solution)/shard_map/ppermute | solution.py:485
  5.5 4.3 %copy-start.1 = (s32[12]{0:T(128)}, s32[12]{0:T(128)S(1)}, u32[]{:S(2)}) copy-start(s32[12]{0:T(128)S(1)} %pad_add_fusion.own_ref) | copy-start | bytes 148
  5.5 4.3 %collective-permute-start = (s32[12]{0:T(128)S(1)}, s32[12]{0:T(128)S(1)}, u32[]{:S(2)}, u32[]{:S(2)}) collective-permute-start(s32[12]{0:T(128)S(1)} %pad_add_fusion.own_ref), channel_id=1, source_target_pairs={{0,4},{4,8},{8,12},{1,5},{5,9},{9,13},{2,6},{6,10},{10,14},{3,7},{... | collective-permute-start | bytes 152 | tf_op jit(solution)/shard_map/ppermute | solution.py:485
  9.8 0.6 copy-start.2
  54.2 0.7 copy-start

commit v3 on v2

--- a/solution.py
+++ b/solution.py
@@ -52,19 +52,28 @@
     return high, low
 
 
-def sandwich(left_ref, right_ref, wave_real, wave_imag):
-    side = wave_real.shape[0]
-    high, low = halves(jnp.concatenate([wave_real, wave_imag], axis=1))
+def sandwich(left_ref, right_ref, waves):
+    side = waves[0][0].shape[0]
+    high, low = halves(
+        jnp.concatenate([jnp.concatenate([re, im], axis=1) for re, im in waves], axis=0)
+    )
     beside = jnp.dot(
         jnp.concatenate([high, low, high], axis=1), right_ref[...],
         preferred_element_type=jnp.float32,
     )
-    high, low = halves(jnp.concatenate([beside[:, :side], beside[:, side:]], axis=0))
+    columns = []
+    for i in range(len(waves)):
+        own = beside[i * side : (i + 1) * side]
+        columns.append(jnp.concatenate([own[:, :side], own[:, side:]], axis=0))
+    high, low = halves(jnp.concatenate(columns, axis=1) if len(columns) > 1 else columns[0])
     stacked = jnp.dot(
         left_ref[...], jnp.concatenate([high, low, high], axis=0),
         preferred_element_type=jnp.float32,
     )
-    return stacked[:side], stacked[side:]
+    return [
+        (stacked[:side, i * side : (i + 1) * side], stacked[side:, i * side : (i + 1) * side])
+        for i in range(len(waves))
+    ]
 
 
 def cos_sin(angle):
@@ -89,28 +98,26 @@
     return pl.multiple_of(jnp.minimum(col // side, cols // side - 2) * side, side)
 
 
-def cut_kernel(own_ref, above_ref, phase_ref, absorb_ref, own_out, above_out, tall):
-    windows, layers, _, side, _ = own_out.shape
+def cut_kernel(above, index_ref, phase_ref, absorb_ref, out_ref, tall):
+    windows, layers, _, side, _ = out_ref.shape
     cols = phase_ref.shape[2]
     for layer in range(layers):
         for which, source in enumerate((phase_ref, absorb_ref)):
-            blank = jnp.zeros((side, cols), jnp.float32)
-            tall[layer, which, :side] = blank
-            tall[layer, which, side : 2 * side] = source[layer]
-            tall[layer, which, 2 * side :] = blank
+            parts = [source[layer], jnp.zeros((side, cols), jnp.float32)]
+            tall[layer, which, :side] = parts[above]
+            tall[layer, which, side:] = parts[1 - above]
 
     def one(w, carried):
-        for index_ref, out_ref, start in ((own_ref, own_out, side), (above_ref, above_out, 0)):
-            row, col = index_ref[w], index_ref[windows + w]
-            base = column_base(col, side, cols)
-            shift = lax.rem(2 * side - (col - base), 2 * side)
-            top = pl.multiple_of(row // 8 * 8, 8)
-            lift = lax.rem(side + 8 - (row - top), side + 8)
-            for layer in range(layers):
-                for which in range(2):
-                    wide = tall[layer, which, pl.ds(start + top, side + 8), pl.ds(base, 2 * side)]
-                    narrow = pltpu.roll(wide, shift, 1)[:, :side]
-                    out_ref[w, layer, which] = pltpu.roll(narrow, lift, 0)[:side]
+        row, col = index_ref[w], index_ref[windows + w]
+        base = column_base(col, side, cols)
+        shift = lax.rem(2 * side - (col - base), 2 * side)
+        top = pl.multiple_of(row // 8 * 8, 8)
+        lift = lax.rem(side + 8 - (row - top), side + 8)
+        for layer in range(layers):
+            for which in range(2):
+                wide = tall[layer, which, pl.ds(top, side + 8), pl.ds(base, 2 * side)]
+                narrow = pltpu.roll(wide, shift, 1)[:, :side]
+                out_ref[w, layer, which] = pltpu.roll(narrow, lift, 0)[:side]
         return carried
 
     lax.fori_loop(0, windows, one, 0)
@@ -171,14 +178,20 @@
 def slot_plan(windows, slabs):
     moved = windows // 2
     kept = windows - moved
-    return kept, moved, -(-(windows + moved) // slabs)
-
-
-def gather_kernel(own, above, patches, from_below, from_above, merged, zs_sem, zr_sem, xs_sem, xr_sem):
+    homes = [(k % slabs, k // slabs) for k in range(windows + moved)]
+    if windows % slabs == 0 and 0 < moved <= slabs:
+        homes[windows:] = [(j * (slabs // moved), windows // slabs) for j in range(moved)]
+    return kept, moved, homes, 1 + max(home[1] for home in homes)
+
+
+def gather_kernel(
+    own, above, measured, patches, measured_above,
+    from_below, from_above, merged, zs_sem, zr_sem, xs_sem, xr_sem, ms_sem, mr_sem,
+):
     windows, layers = own.shape[:2]
     slab, slabs = lax.axis_index("slab"), lax.axis_size("slab")
     tile, tiles = lax.axis_index("tile"), lax.axis_size("tile")
-    kept, moved, _ = slot_plan(windows, slabs)
+    kept, moved, homes, _ = slot_plan(windows, slabs)
     first, last = tile == 0, tile == tiles - 1
     greet()
 
@@ -192,10 +205,15 @@
             src_ref=own.at[kept + j, l], dst_ref=from_above.at[j, l], send_sem=zs_sem.at[kept + j, l],
             recv_sem=zr_sem.at[kept + j, l], device_id={"tile": tile + 1}, device_id_type=MESH)
 
+    def data_down(j):
+        return pltpu.make_async_remote_copy(
+            src_ref=measured.at[kept + j], dst_ref=measured_above.at[j], send_sem=ms_sem.at[j],
+            recv_sem=mr_sem.at[j], device_id={"tile": tile + 1}, device_id_type=MESH)
+
     def across(k, source, l, sender):
         return pltpu.make_async_remote_copy(
-            src_ref=source, dst_ref=patches.at[k // slabs, sender * layers + l], send_sem=xs_sem.at[k, l],
-            recv_sem=xr_sem.at[k // slabs, sender, l], device_id={"slab": k % slabs}, device_id_type=MESH)
+            src_ref=source, dst_ref=patches.at[homes[k][1], sender * layers + l], send_sem=xs_sem.at[k, l],
+            recv_sem=xr_sem.at[homes[k][1], sender, l], device_id={"slab": homes[k][0]}, device_id_type=MESH)
 
     @pl.loop(0, layers)
     def _(l):
@@ -209,14 +227,19 @@
             for j in range(moved):
                 down(j, l).start()
 
+    for j in range(moved):
+        @pl.when(jnp.logical_not(last) & (slab == homes[kept + j][0]))
+        def _():
+            data_down(j).start()
+
     def hand_over(k, source, l):
-        @pl.when(slab != k % slabs)
+        @pl.when(slab != homes[k][0])
         def _():
             across(k, source, l, slab).start()
 
-        @pl.when(slab == k % slabs)
-        def _():
-            patches[k // slabs, slab * layers + l] = source[...]
+        @pl.when(slab == homes[k][0])
+        def _():
+            patches[homes[k][1], slab * layers + l] = source[...]
 
     @pl.when(last)
     def _():
@@ -246,14 +269,23 @@
                 merged[kept + j, l] = above[kept + j, l] + from_above[j, l]
                 hand_over(kept + j, merged.at[kept + j, l], l)
 
+    for j in range(moved):
+        @pl.when(jnp.logical_not(last) & (slab == homes[kept + j][0]))
+        def _():
+            data_down(j).wait_send()
+
+        @pl.when(jnp.logical_not(first) & (slab == homes[kept + j][0]))
+        def _():
+            data_down(j).wait_recv()
+
     def finish(k, source):
-        @pl.when(slab != k % slabs)
+        @pl.when(slab != homes[k][0])
         def _():
             @pl.loop(0, layers)
             def _(l):
                 across(k, source.at[l], l, slab).wait_send()
 
-        @pl.when(slab == k % slabs)
+        @pl.when(slab == homes[k][0])
         def _():
             for sender in range(slabs):
                 @pl.when(sender != slab)
@@ -292,7 +324,7 @@
     windows, layers = own.shape[:2]
     slab, slabs = lax.axis_index("slab"), lax.axis_size("slab")
     tile, tiles = lax.axis_index("tile"), lax.axis_size("tile")
-    kept, moved, _ = slot_plan(windows, slabs)
+    kept, moved, homes, _ = slot_plan(windows, slabs)
     first, last = tile == 0, tile == tiles - 1
     greet()
 
@@ -306,8 +338,8 @@
     def across(k, l, target):
         place, sem = home(k, l)
         return pltpu.make_async_remote_copy(
-            src_ref=grads.at[k // slabs, target * layers + l], dst_ref=place,
-            send_sem=xs_sem.at[k // slabs, target, l], recv_sem=sem,
+            src_ref=grads.at[homes[k][1], target * layers + l], dst_ref=place,
+            send_sem=xs_sem.at[homes[k][1], target, l], recv_sem=sem,
             device_id={"slab": target}, device_id_type=MESH)
 
     def down(i, l):
@@ -321,14 +353,14 @@
             recv_sem=own_sem.at[k, l], device_id={"tile": tile - 1}, device_id_type=MESH)
 
     def give(k, l):
-        @pl.when(slab == k % slabs)
+        @pl.when(slab == homes[k][0])
         def _():
             for target in range(slabs):
                 @pl.when(slab != target)
                 def _():
                     across(k, l, target).start()
 
-            home(k, l)[0][...] = grads[k // slabs, slab * layers + l]
+            home(k, l)[0][...] = grads[homes[k][1], slab * layers + l]
 
     @pl.loop(0, layers)
     def _(l):
@@ -346,7 +378,7 @@
                 give(k, l)
 
     def arrive(k, l):
-        @pl.when(slab != k % slabs)
+        @pl.when(slab != homes[k][0])
         def _():
             across(k, l, slab).wait_recv()
 
@@ -366,7 +398,7 @@
                 up(k, l).start()
 
     def sent(k, l):
-        @pl.when(slab == k % slabs)
+        @pl.when(slab == homes[k][0])
         def _():
             for target in range(slabs):
                 @pl.when(slab != target)
@@ -409,36 +441,42 @@
     windows = measured_ref.shape[0]
     slab, slabs = lax.axis_index("slab"), lax.axis_size("slab")
     tile, tiles = lax.axis_index("tile"), lax.axis_size("tile")
-    kept, moved, _ = slot_plan(windows, slabs)
+    kept, moved, homes, _ = slot_plan(windows, slabs)
+
+    def slot_at(d):
+        slot = jnp.int32(-1)
+        for k, (home_slab, home_depth) in enumerate(homes):
+            if home_depth == d:
+                slot = jnp.where(slab == home_slab, k, slot)
+        return slot
 
     def valid(d):
-        k = d * slabs + slab
-        mine = k < kept
+        k = slot_at(d)
+        mine = (k >= 0) & (k < kept)
         from_above = (k >= kept) & (k < windows) & (tile > 0)
-        extra = (k >= windows) & (k < windows + moved) & (tile == tiles - 1)
+        extra = (k >= windows) & (tile == tiles - 1)
         return mine | from_above | extra
 
-    def far_side(d, wave):
-        k = d * slabs + slab
+    def excess_wave(d, wave):
+        k = slot_at(d)
         is_above = (k >= kept) & (k < windows)
         own_at = jnp.clip(jnp.where(k < windows, k, k - moved), 0, windows - 1)
         above_at = jnp.clip(k, kept, windows - 1)
         live = jnp.where(is_above, above_ref[2 * windows + above_at], own_ref[2 * windows + own_at])
         target = jnp.where(is_above, above_measured_ref[above_at - kept], measured_ref[own_at])
-        far_real, far_imag = sandwich(f_left, f_right, *wave)
+        far_real, far_imag = wave
         excess = (0.5 * live.astype(jnp.float32)) * (far_real * far_real + far_imag * far_imag - target)
-        return sandwich(fa_left, fa_right, excess * far_real, excess * far_imag)
+        return excess * far_real, excess * far_imag
 
     def run(slots):
-        def prepare(s, carried):
+        def prepare(s):
             for d in slots:
                 damping = jnp.exp(-patches[d, s, 1])
                 cos_part, sin_part = cos_sin(patches[d, s, 0])
                 trans[d, s, 0] = damping * cos_part
                 trans[d, s, 1] = damping * sin_part
-            return carried
-
-        lax.fori_loop(0, total, prepare, 0)
+
+        prepare(0)
 
         def forward(s, waves):
             entering = []
@@ -449,15 +487,19 @@
                 mixed[d, s, 0] = mixed_real
                 mixed[d, s, 1] = mixed_imag
                 entering.append((mixed_real, mixed_imag))
-            return tuple(sandwich(q_left, q_right, *wave) for wave in entering)
+            leaving = sandwich(q_left, q_right, entering)
+            prepare(jnp.minimum(s + 1, total - 1))
+            return tuple(leaving)
 
         waves = lax.fori_loop(0, total, forward, tuple((probe_ref[0], probe_ref[1]) for d in slots))
-        backs = tuple(far_side(d, wave) for d, wave in zip(slots, waves))
+        far = sandwich(f_left, f_right, waves)
+        seeds = [excess_wave(d, wave) for d, wave in zip(slots, far)]
+        backs = tuple(sandwich(fa_left, fa_right, seeds))
 
         def backward(i, backs):
             s = total - 1 - i
             result = []
-            for d, (m_real, m_imag) in zip(slots, [sandwich(qa_left, qa_right, *back) for back in backs]):
+            for d, (m_real, m_imag) in zip(slots, sandwich(qa_left, qa_right, backs)):
                 u_real, u_imag = mixed[d, s, 0], mixed[d, s, 1]
                 t_real, t_imag = trans[d, s, 0], trans[d, s, 1]
                 grads[d, s, 0] = u_real * m_imag - u_imag * m_real
@@ -494,7 +536,7 @@
     side = probe_wave.shape[2]
     windows = measured.shape[0]
     slabs = lax.axis_size("slab")
-    kept, moved, depth = slot_plan(windows, slabs)
+    kept, moved, homes, depth = slot_plan(windows, slabs)
     smem = pl.BlockSpec(memory_space=pltpu.SMEM)
     vmem = pl.BlockSpec(memory_space=pltpu.VMEM)
     f32 = jnp.float32
@@ -504,21 +546,26 @@
 
     index_own = jnp.concatenate([rows_at, cols_at, live_mask])
     index_above = passed_along(index_own, "tile", 1)
-    measured_above = passed_along(measured[kept:], "tile", 1)
-    own, above = pl.pallas_call(
-        cut_kernel,
-        out_shape=(pieces, pieces),
-        in_specs=[smem, smem, vmem, vmem],
+    own, above = (
+        pl.pallas_call(
+            functools.partial(cut_kernel, which),
+            out_shape=pieces,
+            in_specs=[smem, vmem, vmem],
+            out_specs=vmem,
+            scratch_shapes=[pltpu.VMEM((layers, 2, 2 * side, cols), f32)],
+            compiler_params=params(),
+            cost_estimate=pl.CostEstimate(
+                flops=0, bytes_accessed=8 * layers * side * (cols + windows * side), transcendentals=0
+            ),
+            name=name,
+        )(index, phase_map, absorption)
+        for which, name, index in ((0, "cut_own", index_own), (1, "cut_above", index_above))
+    )
+    patches, measured_above = pl.pallas_call(
+        gather_kernel,
+        out_shape=(stacked, jax.ShapeDtypeStruct((moved, side, side), f32)),
+        in_specs=[vmem, vmem, vmem],
         out_specs=(vmem, vmem),
-        scratch_shapes=[pltpu.VMEM((layers, 2, 3 * side, cols), f32)],
-        compiler_params=params(),
-        name="cut",
-    )(index_own, index_above, phase_map, absorption)
-    patches = pl.pallas_call(
-        gather_kernel,
-        out_shape=stacked,
-        in_specs=[vmem, vmem],
-        out_specs=vmem,
         scratch_shapes=[
             pltpu.VMEM((kept,) + pieces.shape[1:], f32),
             pltpu.VMEM((moved,) + pieces.shape[1:], f32),
@@ -527,10 +574,12 @@
             dma((windows, layers)),
             dma((windows + moved, layers)),
             dma((depth, slabs, layers)),
+            dma((moved,)),
+            dma((moved,)),
         ],
         compiler_params=params(collective_id=0, has_side_effects=True),
         name="gather",
-    )(own, above)
+    )(own, above, measured)
 
     mats = [jnp.asarray(m) for m in tables(side)]
     grads = pl.pallas_call(

time: 168 us -> 140 us (0.83)
  Pallas kernels: 156 us -> 134 us
  waiting for transfers between devices: 2.36 us -> 0.01 us
  starting transfers between devices: 5.11 us -> 3.19 us
    pallas_call x1, Pallas kernels: 80.9 us -> 56.6 us  [local(): pl.pallas_call(scatter_kernel, out_shape=(pieces, pieces), in_specs=[vmem...]
    ppermute x2 -> x1, waiting for transfers between devices: 2.36 us -> 0.01 us  [passed_along(): return lax.ppermute(array, axis, pairs)]
    ppermute x2 -> x1, starting transfers between devices: 5.11 us -> 3.19 us  [passed_along(): return lax.ppermute(array, axis, pairs)]
    pallas_call x2 -> x3, Pallas kernels: 43.8 us -> 45.7 us  [the longest x1 36.4 us: local(): pl.pallas_call(gather_kernel, out_shape=(stacked, jax.ShapeDtypeStruct((m...]
  transfers between devices with their start and end apart: 2 -> 1, of which waited for: 1 -> 0; matrix products, arithmetic and copies ran while one was open for 0% -> 0% of each run, Pallas kernels for 26% -> 3%
where the time goes in v3:
time: 140 us; the launch traced here: 139 us
  Pallas kernels  134 us (96%)
  starting transfers between devices  3.19 us (2%)
    pallas_call x1, Pallas kernels, local(): pl.pallas_call(scatter_kernel, out_shape=(pieces, pieces), in_specs=[vmem...  56.6 us
    pallas_call x1, Pallas kernels, local(): pl.pallas_call(gather_kernel, out_shape=(stacked, jax.ShapeDtypeStruct((m...  36.4 us
    pallas_call x1, Pallas kernels, local(): pl.pallas_call(wave_kernel, out_shape=stacked, in_specs=[smem, smem] + [v...  25.2 us
    pallas_call x2, Pallas kernels, local(): pl.pallas_call(functools.partial(cut_kernel, which), out_shape=pieces, in...  9.34 us
    pallas_call x1, Pallas kernels, local(): pl.pallas_call(place_kernel, out_shape=(whole, whole), in_specs=[smem, sm...  6.38 us
    ppermute x1, starting transfers between devices, passed_along(): return lax.ppermute(array, axis, pairs)  3.19 us
  transfers between devices with their start and end apart: 1, of which 0 were waited for; matrix products, arithmetic and copies ran while one was open for 0% of the time, Pallas kernels for 3%

profile of v3, /device:TPU:19, one launch (start us, length us, event | category | flops | bytes accessed | tf_op | source)
XLA Modules:
  0.0 139.1 jit_solution(18411093763620357206)
XLA Ops:
  0.6 0.8 pad_add_fusion.index_ref.own_ref
  1.4 0.0 copy-start
  1.4 3.2 %collective-permute-start = (s32[12]{0:T(128)S(1)}, s32[12]{0:T(128)S(1)}, u32[]{:S(2)}, u32[]{:S(2)}) collective-permute-start(s32[12]{0:T(128)S(1)} %pad_add_fusion.index_ref.own_ref), channel_id=1, source_target_pairs={{0,4},{4,8},{8,12},{1,5},{5,9},{9,13},{2,6},{6,10},{10,14},{3,7},{... | collective-permute-start | bytes 152 | tf_op jit(solution)/shard_map/ppermute | solution.py:527
  4.6 0.0 copy-done
  4.6 4.7 %cut_own.1.own = f32[4,4,2,128,128]{4,3,2,1,0:T(8,128)} custom-call(s32[12]{0:T(128)} %copy-done, f32[4,128,512]{2,1,0:T(8,128)} %phase_ref.3, f32[4,128,512]{2,1,0:T(8,128)} %absorb_ref.3), custom_call_target="tpu_custom_call" | custom-call | bytes 4194304 | tf_op jit(solution)/shard_map/cut_own/pallas_call | solution.py:550
  9.3 0.0 collective-permute-done.index_ref.above_ref
  9.3 0.0 copy-start.1
  9.3 0.6 copy-done.1
  9.8 4.7 %cut_above.1.above = f32[4,4,2,128,128]{4,3,2,1,0:T(8,128)} custom-call(s32[12]{0:T(128)} %copy-done.1, f32[4,128,512]{2,1,0:T(8,128)} %phase_ref.3, f32[4,128,512]{2,1,0:T(8,128)} %absorb_ref.3), custom_call_target="tpu_custom_call" | custom-call | bytes 4194304 | tf_op jit(solution)/shard_map/cut_above/pallas_call | solution.py:550
  14.5 36.4 %gather.1 = (f32[2,16,2,128,128]{4,3,2,1,0:T(8,128)}, f32[2,128,128]{2,1,0:T(8,128)}) custom-call(f32[4,4,2,128,128]{4,3,2,1,0:T(8,128)} %cut_own.1.own, f32[4,4,2,128,128]{4,3,2,1,0:T(8,128)} %cut_above.1.above, f32[4,128,128]{2,1,0:T(8,128)} %measured_ref.1), custom_call_target="tpu_custom_call" | custom-call | tf_op jit(solution)/shard_map/gather/pallas_call | solution.py:564
  50.9 25.2 %waves.1.grads = f32[2,16,2,128,128]{4,3,2,1,0:T(8,128)} custom-call(s32[12]{0:T(128)} %copy-done, s32[12]{0:T(128)} %copy-done.1, f32[2,16,2,128,128]{4,3,2,1,0:T(8,128)} %get-tuple-element.6.patches, f32[2,128,128]{2,1,0:T(8,128)} %probe_ref.1, f32[4,128,128]{2,1,0:T(8,128)} %measured_ref.1, f32[2,128,128]{2,1,0:T(8,128)} %get-tuple-element.7.above_measured_ref, ...), custom_call_target="tpu_custom_call" | custom-call | tf_op jit(solution)/shard_map/waves/pallas_call | solution.py:585
  76.1 56.6 %scatter.1 = (f32[4,4,2,128,128]{4,3,2,1,0:T(8,128)}, f32[4,4,2,128,128]{4,3,2,1,0:T(8,128)}) custom-call(f32[2,16,2,128,128]{4,3,2,1,0:T(8,128)} %waves.1.grads), custom_call_target="tpu_custom_call" | custom-call | tf_op jit(solution)/shard_map/scatter/pallas_call | solution.py:595
  132.7 6.4 %place.1 = (f32[4,128,512]{2,1,0:T(8,128)}, f32[4,128,512]{2,1,0:T(8,128)}) custom-call(s32[12]{0:T(128)} %copy-done, s32[12]{0:T(128)} %copy-done.1, f32[4,4,2,128,128]{4,3,2,1,0:T(8,128)} %get-tuple-element.8.own_pieces, f32[4,4,2,128,128]{4,3,2,1,0:T(8,128)} %get-tuple-element.9.above_pieces), custom_call_target="tpu_custom_call" | custom-call | tf_op jit(solution)/shard_map/place/pallas_call | solution.py:610
Async XLA Ops:
  1.4 3.2 %copy-start = (s32[12]{0:T(128)}, s32[12]{0:T(128)S(1)}, u32[]{:S(2)}) copy-start(s32[12]{0:T(128)S(1)} %pad_add_fusion.index_ref.own_ref) | copy-start | bytes 148
  1.4 7.9 %collective-permute-start = (s32[12]{0:T(128)S(1)}, s32[12]{0:T(128)S(1)}, u32[]{:S(2)}, u32[]{:S(2)}) collective-permute-start(s32[12]{0:T(128)S(1)} %pad_add_fusion.index_ref.own_ref), channel_id=1, source_target_pairs={{0,4},{4,8},{8,12},{1,5},{5,9},{9,13},{2,6},{6,10},{10,14},{3,7},{... | collective-permute-start | bytes 152 | tf_op jit(solution)/shard_map/ppermute | solution.py:527
  9.3 0.6 copy-start.1

commit v4 on v3

--- a/solution.py
+++ b/solution.py
@@ -178,10 +178,9 @@
 def slot_plan(windows, slabs):
     moved = windows // 2
     kept = windows - moved
-    homes = [(k % slabs, k // slabs) for k in range(windows + moved)]
-    if windows % slabs == 0 and 0 < moved <= slabs:
-        homes[windows:] = [(j * (slabs // moved), windows // slabs) for j in range(moved)]
-    return kept, moved, homes, 1 + max(home[1] for home in homes)
+    lanes = slabs // 2
+    homes = [(k % lanes, k // lanes) for k in range(windows + moved)]
+    return kept, moved, homes, 1 + max(home[1] for home in homes), lanes
 
 
 def gather_kernel(
@@ -191,7 +190,8 @@
     windows, layers = own.shape[:2]
     slab, slabs = lax.axis_index("slab"), lax.axis_size("slab")
     tile, tiles = lax.axis_index("tile"), lax.axis_size("tile")
-    kept, moved, homes, _ = slot_plan(windows, slabs)
+    kept, moved, homes, _, lanes = slot_plan(windows, slabs)
+    half, lane = slab // lanes, lax.rem(slab, lanes)
     first, last = tile == 0, tile == tiles - 1
     greet()
 
@@ -213,7 +213,7 @@
     def across(k, source, l, sender):
         return pltpu.make_async_remote_copy(
             src_ref=source, dst_ref=patches.at[homes[k][1], sender * layers + l], send_sem=xs_sem.at[k, l],
-            recv_sem=xr_sem.at[homes[k][1], sender, l], device_id={"slab": homes[k][0]}, device_id_type=MESH)
+            recv_sem=xr_sem.at[homes[k][1], sender, l], device_id={"slab": half * lanes + homes[k][0]}, device_id_type=MESH)
 
     @pl.loop(0, layers)
     def _(l):
@@ -228,18 +228,18 @@
                 down(j, l).start()
 
     for j in range(moved):
-        @pl.when(jnp.logical_not(last) & (slab == homes[kept + j][0]))
+        @pl.when(jnp.logical_not(last) & (lane == homes[kept + j][0]))
         def _():
             data_down(j).start()
 
     def hand_over(k, source, l):
-        @pl.when(slab != homes[k][0])
-        def _():
-            across(k, source, l, slab).start()
-
-        @pl.when(slab == homes[k][0])
-        def _():
-            patches[homes[k][1], slab * layers + l] = source[...]
+        @pl.when(lane != homes[k][0])
+        def _():
+            across(k, source, l, lane).start()
+
+        @pl.when(lane == homes[k][0])
+        def _():
+            patches[homes[k][1], lane * layers + l] = source[...]
 
     @pl.when(last)
     def _():
@@ -270,25 +270,25 @@
                 hand_over(kept + j, merged.at[kept + j, l], l)
 
     for j in range(moved):
-        @pl.when(jnp.logical_not(last) & (slab == homes[kept + j][0]))
+        @pl.when(jnp.logical_not(last) & (lane == homes[kept + j][0]))
         def _():
             data_down(j).wait_send()
 
-        @pl.when(jnp.logical_not(first) & (slab == homes[kept + j][0]))
+        @pl.when(jnp.logical_not(first) & (lane == homes[kept + j][0]))
         def _():
             data_down(j).wait_recv()
 
     def finish(k, source):
-        @pl.when(slab != homes[k][0])
+        @pl.when(lane != homes[k][0])
         def _():
             @pl.loop(0, layers)
             def _(l):
-                across(k, source.at[l], l, slab).wait_send()
-
-        @pl.when(slab == homes[k][0])
-        def _():
-            for sender in range(slabs):
-                @pl.when(sender != slab)
+                across(k, source.at[l], l, lane).wait_send()
+
+        @pl.when(lane == homes[k][0])
+        def _():
+            for sender in range(lanes):
+                @pl.when(sender != lane)
                 def _():
                     @pl.loop(0, layers)
                     def _(l):
@@ -324,7 +324,8 @@
     windows, layers = own.shape[:2]
     slab, slabs = lax.axis_index("slab"), lax.axis_size("slab")
     tile, tiles = lax.axis_index("tile"), lax.axis_size("tile")
-    kept, moved, homes, _ = slot_plan(windows, slabs)
+    kept, moved, homes, _, lanes = slot_plan(windows, slabs)
+    half, lane = slab // lanes, lax.rem(slab, lanes)
     first, last = tile == 0, tile == tiles - 1
     greet()
 
@@ -340,7 +341,7 @@
         return pltpu.make_async_remote_copy(
             src_ref=grads.at[homes[k][1], target * layers + l], dst_ref=place,
             send_sem=xs_sem.at[homes[k][1], target, l], recv_sem=sem,
-            device_id={"slab": target}, device_id_type=MESH)
+            device_id={"slab": half * lanes + target}, device_id_type=MESH)
 
     def down(i, l):
         return pltpu.make_async_remote_copy(
@@ -353,14 +354,14 @@
             recv_sem=own_sem.at[k, l], device_id={"tile": tile - 1}, device_id_type=MESH)
 
     def give(k, l):
-        @pl.when(slab == homes[k][0])
-        def _():
-            for target in range(slabs):
-                @pl.when(slab != target)
+        @pl.when(lane == homes[k][0])
+        def _():
+            for target in range(lanes):
+                @pl.when(lane != target)
                 def _():
                     across(k, l, target).start()
 
-            home(k, l)[0][...] = grads[homes[k][1], slab * layers + l]
+            home(k, l)[0][...] = grads[homes[k][1], lane * layers + l]
 
     @pl.loop(0, layers)
     def _(l):
@@ -378,9 +379,9 @@
                 give(k, l)
 
     def arrive(k, l):
-        @pl.when(slab != homes[k][0])
-        def _():
-            across(k, l, slab).wait_recv()
+        @pl.when(lane != homes[k][0])
+        def _():
+            across(k, l, lane).wait_recv()
 
     @pl.loop(0, layers)
     def _(l):
@@ -398,10 +399,10 @@
                 up(k, l).start()
 
     def sent(k, l):
-        @pl.when(slab == homes[k][0])
-        def _():
-            for target in range(slabs):
-                @pl.when(slab != target)
+        @pl.when(lane == homes[k][0])
+        def _():
+            for target in range(lanes):
+                @pl.when(lane != target)
                 def _():
                     across(k, l, target).wait_send()
 
@@ -435,19 +436,20 @@
 def wave_kernel(
     own_ref, above_ref, patches, probe_ref, measured_ref, above_measured_ref,
     q_left, q_right, qa_left, qa_right, f_left, f_right, fa_left, fa_right,
-    grads, trans, mixed,
+    grads, trans, mixed, leaving, arriving, send_sem, recv_sem,
 ):
     depth, total, _, side, _ = patches.shape
     windows = measured_ref.shape[0]
     slab, slabs = lax.axis_index("slab"), lax.axis_size("slab")
     tile, tiles = lax.axis_index("tile"), lax.axis_size("tile")
-    kept, moved, homes, _ = slot_plan(windows, slabs)
+    kept, moved, homes, _, lanes = slot_plan(windows, slabs)
+    half, lane = slab // lanes, lax.rem(slab, lanes)
 
     def slot_at(d):
         slot = jnp.int32(-1)
         for k, (home_slab, home_depth) in enumerate(homes):
             if home_depth == d:
-                slot = jnp.where(slab == home_slab, k, slot)
+                slot = jnp.where(lane == home_slab, k, slot)
         return slot
 
     def valid(d):
@@ -491,10 +493,24 @@
             prepare(jnp.minimum(s + 1, total - 1))
             return tuple(leaving)
 
-        waves = lax.fori_loop(0, total, forward, tuple((probe_ref[0], probe_ref[1]) for d in slots))
-        far = sandwich(f_left, f_right, waves)
-        seeds = [excess_wave(d, wave) for d, wave in zip(slots, far)]
-        backs = tuple(sandwich(fa_left, fa_right, seeds))
+        def hop(target):
+            return [
+                pltpu.make_async_remote_copy(
+                    src_ref=leaving.at[d], dst_ref=arriving.at[d], send_sem=send_sem.at[d],
+                    recv_sem=recv_sem.at[d], device_id={"slab": target}, device_id_type=MESH)
+                for d in slots
+            ]
+
+        def pass_on(waves, target):
+            for d, wave, copy in zip(slots, waves, hop(target)):
+                leaving[d, 0] = wave[0]
+                leaving[d, 1] = wave[1]
+                copy.start()
+
+        def arrived():
+            for copy in hop(other):
+                copy.wait_recv()
+            return tuple((arriving[d, 0], arriving[d, 1]) for d in slots)
 
         def backward(i, backs):
             s = total - 1 - i
@@ -507,18 +523,35 @@
                 result.append((t_real * m_real + t_imag * m_imag, t_real * m_imag - t_imag * m_real))
             return tuple(result)
 
-        lax.fori_loop(0, total, backward, backs)
-
-    deeper = valid(1) if depth > 1 else jnp.bool_(False)
-
-    @pl.when(valid(0) & jnp.logical_not(deeper))
-    def _():
-        run([0])
-
-    if depth > 1:
-        @pl.when(deeper)
-        def _():
-            run(list(range(depth)))
+        @pl.when(half == 0)
+        def _():
+            start = tuple((probe_ref[0], probe_ref[1]) for d in slots)
+            pass_on(lax.fori_loop(0, total, forward, start), other)
+            backs = arrived()
+            lax.fori_loop(0, total, backward, backs)
+
+        @pl.when(half == 1)
+        def _():
+            waves = lax.fori_loop(0, total, forward, arrived())
+            far = sandwich(f_left, f_right, waves)
+            seeds = [excess_wave(d, wave) for d, wave in zip(slots, far)]
+            backs = tuple(sandwich(fa_left, fa_right, seeds))
+            pass_on(lax.fori_loop(0, total, backward, backs), other)
+
+        for copy in hop(other):
+            copy.wait_send()
+
+    other = jnp.where(half == 0, slab + lanes, slab - lanes)
+    barrier = pltpu.get_barrier_semaphore()
+    pl.semaphore_signal(barrier, inc=1, device_id={"slab": other}, device_id_type=MESH)
+    pl.semaphore_wait(barrier, 1)
+    filled = jnp.int32(0)
+    for d in range(depth):
+        filled = jnp.where(valid(d), d + 1, filled)
+    for count in range(1, depth + 1):
+        @pl.when(filled == count)
+        def _():
+            run(list(range(count)))
 
 
 def passed_along(array, axis, by):
@@ -536,13 +569,13 @@
     side = probe_wave.shape[2]
     windows = measured.shape[0]
     slabs = lax.axis_size("slab")
-    kept, moved, homes, depth = slot_plan(windows, slabs)
+    kept, moved, homes, depth, lanes = slot_plan(windows, slabs)
     smem = pl.BlockSpec(memory_space=pltpu.SMEM)
     vmem = pl.BlockSpec(memory_space=pltpu.VMEM)
     f32 = jnp.float32
     dma = pltpu.SemaphoreType.DMA
     pieces = jax.ShapeDtypeStruct((windows, layers, 2, side, side), f32)
-    stacked = jax.ShapeDtypeStruct((depth, slabs * layers, 2, side, side), f32)
+    stacked = jax.ShapeDtypeStruct((depth, lanes * layers, 2, side, side), f32)
 
     index_own = jnp.concatenate([rows_at, cols_at, live_mask])
     index_above = passed_along(index_own, "tile", 1)
@@ -573,7 +606,7 @@
             dma((windows, layers)),
             dma((windows, layers)),
             dma((windows + moved, layers)),
-            dma((depth, slabs, layers)),
+            dma((depth, lanes, layers)),
             dma((moved,)),
             dma((moved,)),
         ],
@@ -587,8 +620,15 @@
         out_shape=stacked,
         in_specs=[smem, smem] + [vmem] * (4 + len(mats)),
         out_specs=vmem,
-        scratch_shapes=[pltpu.VMEM(stacked.shape, f32), pltpu.VMEM(stacked.shape, f32)],
-        compiler_params=params(),
+        scratch_shapes=[
+            pltpu.VMEM(stacked.shape, f32),
+            pltpu.VMEM(stacked.shape, f32),
+            pltpu.VMEM((depth, 2, side, side), f32),
+            pltpu.VMEM((depth, 2, side, side), f32),
+            dma((depth,)),
+            dma((depth,)),
+        ],
+        compiler_params=params(collective_id=2, has_side_effects=True),
         name="waves",
     )(index_own, index_above, patches, probe_wave, measured, measured_above, *mats)
 
@@ -599,7 +639,7 @@
         out_specs=(vmem, vmem),
         scratch_shapes=[
             dma((windows, layers)),
-            dma((depth, slabs, layers)),
+            dma((depth, lanes, layers)),
             dma((windows, layers)),
             dma((windows, layers)),
         ],

time: 140 us -> 149 us (1.064)
  Pallas kernels: 134 us -> 143 us
    pallas_call x1, Pallas kernels: 25.2 us -> 39.3 us  [local(): pl.pallas_call(wave_kernel, out_shape=stacked, in_specs=[smem, smem] + [v...]
    pallas_call x1, Pallas kernels: 36.4 us -> 31.8 us  [local(): pl.pallas_call(gather_kernel, out_shape=(stacked, jax.ShapeDtypeStruct((m...]
where the time goes in v4:
time: 149 us; the launch traced here: 148 us
  Pallas kernels  143 us (96%)
  starting transfers between devices  3.19 us (2%)
    pallas_call x1, Pallas kernels, local(): pl.pallas_call(scatter_kernel, out_shape=(pieces, pieces), in_specs=[vmem...  55.9 us
    pallas_call x1, Pallas kernels, local(): pl.pallas_call(wave_kernel, out_shape=stacked, in_specs=[smem, smem] + [v...  39.3 us
    pallas_call x1, Pallas kernels, local(): pl.pallas_call(gather_kernel, out_shape=(stacked, jax.ShapeDtypeStruct((m...  31.8 us
    pallas_call x2, Pallas kernels, local(): pl.pallas_call(functools.partial(cut_kernel, which), out_shape=pieces, in...  9.39 us
    pallas_call x1, Pallas kernels, local(): pl.pallas_call(place_kernel, out_shape=(whole, whole), in_specs=[smem, sm...  6.38 us
    ppermute x1, starting transfers between devices, passed_along(): return lax.ppermute(array, axis, pairs)  3.19 us
  transfers between devices with their start and end apart: 1, of which 0 were waited for; matrix products, arithmetic and copies ran while one was open for 0% of the time, Pallas kernels for 3%

profile of v4, /device:TPU:19, one launch (start us, length us, event | category | flops | bytes accessed | tf_op | source)
XLA Modules:
  0.0 148.0 jit_solution(9965143734632191155)
XLA Ops:
  0.6 0.8 pad_add_fusion.index_ref.own_ref
  1.4 0.0 copy-start
  1.4 3.2 %collective-permute-start = (s32[12]{0:T(128)S(1)}, s32[12]{0:T(128)S(1)}, u32[]{:S(2)}, u32[]{:S(2)}) collective-permute-start(s32[12]{0:T(128)S(1)} %pad_add_fusion.index_ref.own_ref), channel_id=1, source_target_pairs={{0,4},{4,8},{8,12},{1,5},{5,9},{9,13},{2,6},{6,10},{10,14},{3,7},{... | collective-permute-start | bytes 152 | tf_op jit(solution)/shard_map/ppermute | solution.py:560
  4.6 0.0 copy-done
  4.6 4.7 %cut_own.1.own = f32[4,4,2,128,128]{4,3,2,1,0:T(8,128)} custom-call(s32[12]{0:T(128)} %copy-done, f32[4,128,512]{2,1,0:T(8,128)} %phase_ref.3, f32[4,128,512]{2,1,0:T(8,128)} %absorb_ref.3), custom_call_target="tpu_custom_call" | custom-call | bytes 4194304 | tf_op jit(solution)/shard_map/cut_own/pallas_call | solution.py:583
  9.3 0.0 collective-permute-done.index_ref.above_ref
  9.3 0.0 copy-start.1
  9.3 0.6 copy-done.1
  9.9 4.7 %cut_above.1.above = f32[4,4,2,128,128]{4,3,2,1,0:T(8,128)} custom-call(s32[12]{0:T(128)} %copy-done.1, f32[4,128,512]{2,1,0:T(8,128)} %phase_ref.3, f32[4,128,512]{2,1,0:T(8,128)} %absorb_ref.3), custom_call_target="tpu_custom_call" | custom-call | bytes 4194304 | tf_op jit(solution)/shard_map/cut_above/pallas_call | solution.py:583
  14.6 31.8 %gather.1 = (f32[3,8,2,128,128]{4,3,2,1,0:T(8,128)}, f32[2,128,128]{2,1,0:T(8,128)}) custom-call(f32[4,4,2,128,128]{4,3,2,1,0:T(8,128)} %cut_own.1.own, f32[4,4,2,128,128]{4,3,2,1,0:T(8,128)} %cut_above.1.above, f32[4,128,128]{2,1,0:T(8,128)} %measured_ref.1), custom_call_target="tpu_custom_call" | custom-call | tf_op jit(solution)/shard_map/gather/pallas_call | solution.py:597
  46.4 39.3 %waves.1.grads = f32[3,8,2,128,128]{4,3,2,1,0:T(8,128)} custom-call(s32[12]{0:T(128)} %copy-done, s32[12]{0:T(128)} %copy-done.1, f32[3,8,2,128,128]{4,3,2,1,0:T(8,128)} %get-tuple-element.6.patches, f32[2,128,128]{2,1,0:T(8,128)} %probe_ref.1, f32[4,128,128]{2,1,0:T(8,128)} %measured_ref.1, f32[2,128,128]{2,1,0:T(8,128)} %get-tuple-element.7.above_measured_ref, ...), custom_call_target="tpu_custom_call" | custom-call | tf_op jit(solution)/shard_map/waves/pallas_call | solution.py:618
  85.7 55.9 %scatter.1 = (f32[4,4,2,128,128]{4,3,2,1,0:T(8,128)}, f32[4,4,2,128,128]{4,3,2,1,0:T(8,128)}) custom-call(f32[3,8,2,128,128]{4,3,2,1,0:T(8,128)} %waves.1.grads), custom_call_target="tpu_custom_call" | custom-call | tf_op jit(solution)/shard_map/scatter/pallas_call | solution.py:635
  141.6 6.4 %place.1 = (f32[4,128,512]{2,1,0:T(8,128)}, f32[4,128,512]{2,1,0:T(8,128)}) custom-call(s32[12]{0:T(128)} %copy-done, s32[12]{0:T(128)} %copy-done.1, f32[4,4,2,128,128]{4,3,2,1,0:T(8,128)} %get-tuple-element.8.own_pieces, f32[4,4,2,128,128]{4,3,2,1,0:T(8,128)} %get-tuple-element.9.above_pieces), custom_call_target="tpu_custom_call" | custom-call | tf_op jit(solution)/shard_map/place/pallas_call | solution.py:650
Async XLA Ops:
  1.4 3.2 %copy-start = (s32[12]{0:T(128)}, s32[12]{0:T(128)S(1)}, u32[]{:S(2)}) copy-start(s32[12]{0:T(128)S(1)} %pad_add_fusion.index_ref.own_ref) | copy-start | bytes 148
  1.4 7.9 %collective-permute-start = (s32[12]{0:T(128)S(1)}, s32[12]{0:T(128)S(1)}, u32[]{:S(2)}, u32[]{:S(2)}) collective-permute-start(s32[12]{0:T(128)S(1)} %pad_add_fusion.index_ref.own_ref), channel_id=1, source_target_pairs={{0,4},{4,8},{8,12},{1,5},{5,9},{9,13},{2,6},{6,10},{10,14},{3,7},{... | collective-permute-start | bytes 152 | tf_op jit(solution)/shard_map/ppermute | solution.py:560
  9.3 0.6 copy-start.1

commit v5 on v3

--- a/solution.py
+++ b/solution.py
@@ -320,11 +320,18 @@
                 down(j, l).wait_send()
 
 
-def scatter_kernel(grads, own, above, zs_sem, xs_sem, own_sem, above_sem):
-    windows, layers = own.shape[:2]
+def wave_kernel(
+    own_ref, above_ref, patches, probe_ref, measured_ref, above_measured_ref,
+    q_left, q_right, qa_left, qa_right, f_left, f_right, fa_left, fa_right,
+    own, above, grads, trans, mixed, zs_sem, xs_sem, own_sem, above_sem,
+):
+    depth, total, _, side, _ = patches.shape
+    windows = measured_ref.shape[0]
     slab, slabs = lax.axis_index("slab"), lax.axis_size("slab")
     tile, tiles = lax.axis_index("tile"), lax.axis_size("tile")
     kept, moved, homes, _ = slot_plan(windows, slabs)
+
+    layers = own.shape[1]
     first, last = tile == 0, tile == tiles - 1
     greet()
 
@@ -352,96 +359,22 @@
             src_ref=above.at[k, l], dst_ref=own.at[k, l], send_sem=zs_sem.at[k, l],
             recv_sem=own_sem.at[k, l], device_id={"tile": tile - 1}, device_id_type=MESH)
 
-    def give(k, l):
-        @pl.when(slab == homes[k][0])
-        def _():
-            for target in range(slabs):
-                @pl.when(slab != target)
-                def _():
-                    across(k, l, target).start()
-
-            home(k, l)[0][...] = grads[homes[k][1], slab * layers + l]
-
-    @pl.loop(0, layers)
-    def _(l):
-        for k in range(kept):
-            give(k, l)
-
-        @pl.when(jnp.logical_not(first))
-        def _():
-            for k in range(kept, windows):
-                give(k, l)
-
-        @pl.when(last)
-        def _():
-            for k in range(windows, windows + moved):
-                give(k, l)
-
-    def arrive(k, l):
-        @pl.when(slab != homes[k][0])
-        def _():
-            across(k, l, slab).wait_recv()
-
-    @pl.loop(0, layers)
-    def _(l):
-        for k in range(kept):
-            arrive(k, l)
-
-            @pl.when(jnp.logical_not(last))
-            def _():
-                down(k, l).start()
-
-        @pl.when(jnp.logical_not(first))
-        def _():
-            for k in range(kept, windows):
-                arrive(k, l)
-                up(k, l).start()
-
-    def sent(k, l):
-        @pl.when(slab == homes[k][0])
-        def _():
-            for target in range(slabs):
-                @pl.when(slab != target)
-                def _():
-                    across(k, l, target).wait_send()
-
-    @pl.loop(0, layers)
-    def _(l):
-        for k in range(kept):
-            sent(k, l)
-
-        @pl.when(jnp.logical_not(first))
-        def _():
-            for k in range(kept, windows):
-                sent(k, l)
-                up(k, l).wait_send()
-            for k in range(kept):
-                down(k, l).wait_recv()
-
-        @pl.when(jnp.logical_not(last))
-        def _():
-            for k in range(kept):
-                down(k, l).wait_send()
-            for k in range(kept, windows):
-                up(k, l).wait_recv()
-
-        @pl.when(last)
-        def _():
-            for k in range(windows, windows + moved):
-                arrive(k, l)
-                sent(k, l)
-
-
-def wave_kernel(
-    own_ref, above_ref, patches, probe_ref, measured_ref, above_measured_ref,
-    q_left, q_right, qa_left, qa_right, f_left, f_right, fa_left, fa_right,
-    grads, trans, mixed,
-):
-    depth, total, _, side, _ = patches.shape
-    windows = measured_ref.shape[0]
-    slab, slabs = lax.axis_index("slab"), lax.axis_size("slab")
-    tile, tiles = lax.axis_index("tile"), lax.axis_size("tile")
-    kept, moved, homes, _ = slot_plan(windows, slabs)
+    def give(k, s):
+        target, l = s // layers, lax.rem(s, layers)
+
+        @pl.when(slab != target)
+        def _():
+            across(k, l, target).start()
+
+        @pl.when(slab == target)
+        def _():
+            home(k, l)[0][...] = grads[homes[k][1], s]
+
+    def in_use(k):
+        here = slab == homes[k][0]
+        if k < kept:
+            return here
+        return here & (jnp.logical_not(first) if k < windows else last)
 
     def slot_at(d):
         slot = jnp.int32(-1)
@@ -505,6 +438,12 @@
                 grads[d, s, 0] = u_real * m_imag - u_imag * m_real
                 grads[d, s, 1] = -(u_real * m_real + u_imag * m_imag)
                 result.append((t_real * m_real + t_imag * m_imag, t_real * m_imag - t_imag * m_real))
+            for k, (_, home_depth) in enumerate(homes):
+                if home_depth in slots:
+                    @pl.when(in_use(k))
+                    def _():
+                        give(k, s)
+
             return tuple(result)
 
         lax.fori_loop(0, total, backward, backs)
@@ -519,6 +458,61 @@
         @pl.when(deeper)
         def _():
             run(list(range(depth)))
+
+    def arrive(k, l):
+        @pl.when(slab != homes[k][0])
+        def _():
+            across(k, l, slab).wait_recv()
+
+    @pl.loop(0, layers)
+    def _(back):
+        l = layers - 1 - back
+        for k in range(kept):
+            arrive(k, l)
+
+            @pl.when(jnp.logical_not(last))
+            def _():
+                down(k, l).start()
+
+        @pl.when(jnp.logical_not(first))
+        def _():
+            for k in range(kept, windows):
+                arrive(k, l)
+                up(k, l).start()
+
+    def sent(k, l):
+        @pl.when(slab == homes[k][0])
+        def _():
+            for target in range(slabs):
+                @pl.when(slab != target)
+                def _():
+                    across(k, l, target).wait_send()
+
+    @pl.loop(0, layers)
+    def _(l):
+        for k in range(kept):
+            sent(k, l)
+
+        @pl.when(jnp.logical_not(first))
+        def _():
+            for k in range(kept, windows):
+                sent(k, l)
+                up(k, l).wait_send()
+            for k in range(kept):
+                down(k, l).wait_recv()
+
+        @pl.when(jnp.logical_not(last))
+        def _():
+            for k in range(kept):
+                down(k, l).wait_send()
+            for k in range(kept, windows):
+                up(k, l).wait_recv()
+
+        @pl.when(last)
+        def _():
+            for k in range(windows, windows + moved):
+                arrive(k, l)
+                sent(k, l)
 
 
 def passed_along(array, axis, by):
@@ -582,30 +576,23 @@
     )(own, above, measured)
 
     mats = [jnp.asarray(m) for m in tables(side)]
-    grads = pl.pallas_call(
+    own, above = pl.pallas_call(
         wave_kernel,
-        out_shape=stacked,
+        out_shape=(pieces, pieces),
         in_specs=[smem, smem] + [vmem] * (4 + len(mats)),
-        out_specs=vmem,
-        scratch_shapes=[pltpu.VMEM(stacked.shape, f32), pltpu.VMEM(stacked.shape, f32)],
-        compiler_params=params(),
-        name="waves",
-    )(index_own, index_above, patches, probe_wave, measured, measured_above, *mats)
-
-    own, above = pl.pallas_call(
-        scatter_kernel,
-        out_shape=(pieces, pieces),
-        in_specs=[vmem],
         out_specs=(vmem, vmem),
         scratch_shapes=[
+            pltpu.VMEM(stacked.shape, f32),
+            pltpu.VMEM(stacked.shape, f32),
+            pltpu.VMEM(stacked.shape, f32),
             dma((windows, layers)),
             dma((depth, slabs, layers)),
             dma((windows, layers)),
             dma((windows, layers)),
         ],
         compiler_params=params(collective_id=1, has_side_effects=True),
-        name="scatter",
-    )(grads)
+        name="waves",
+    )(index_own, index_above, patches, probe_wave, measured, measured_above, *mats)
     whole = jax.ShapeDtypeStruct(phase_map.shape, f32)
     return pl.pallas_call(
         place_kernel,

time: 140 us -> 126 us (0.900)
  the two profiles are of different devices: /device:TPU:19 before, /device:TPU:16 now
where the time goes in v5:
time: 126 us; the launch traced here: 125 us
  Pallas kernels  120 us (95%)
  starting transfers between devices  3.47 us (3%)
    pallas_call x1, Pallas kernels, local(): pl.pallas_call(wave_kernel, out_shape=(pieces, pieces), in_specs=[smem, s...  69.1 us
    pallas_call x1, Pallas kernels, local(): pl.pallas_call(gather_kernel, out_shape=(stacked, jax.ShapeDtypeStruct((m...  35.1 us
    pallas_call x2, Pallas kernels, local(): pl.pallas_call(functools.partial(cut_kernel, which), out_shape=pieces, in...  9.34 us
    pallas_call x1, Pallas kernels, local(): pl.pallas_call(place_kernel, out_shape=(whole, whole), in_specs=[smem, sm...  6.39 us
    ppermute x1, starting transfers between devices, passed_along(): return lax.ppermute(array, axis, pairs)  3.47 us
  transfers between devices with their start and end apart: 1, of which 0 were waited for; matrix products, arithmetic and copies ran while one was open for 0% of the time, Pallas kernels for 4%

profile of v5, /device:TPU:16, one launch (start us, length us, event | category | flops | bytes accessed | tf_op | source)
XLA Modules:
  0.0 125.4 jit_solution(8737014911648598709)
XLA Ops:
  0.6 0.8 pad_add_fusion.index_ref.own_ref
  1.4 0.0 copy-start
  1.4 3.5 %collective-permute-start = (s32[12]{0:T(128)S(1)}, s32[12]{0:T(128)S(1)}, u32[]{:S(2)}, u32[]{:S(2)}) collective-permute-start(s32[12]{0:T(128)S(1)} %pad_add_fusion.index_ref.own_ref), channel_id=1, source_target_pairs={{0,4},{4,8},{8,12},{1,5},{5,9},{9,13},{2,6},{6,10},{10,14},{3,7},{... | collective-permute-start | bytes 152 | tf_op jit(solution)/shard_map/ppermute | solution.py:521
  4.9 0.0 copy-done
  4.9 4.7 %cut_own.1.own = f32[4,4,2,128,128]{4,3,2,1,0:T(8,128)} custom-call(s32[12]{0:T(128)} %copy-done, f32[4,128,512]{2,1,0:T(8,128)} %phase_ref.3, f32[4,128,512]{2,1,0:T(8,128)} %absorb_ref.3), custom_call_target="tpu_custom_call" | custom-call | bytes 4194304 | tf_op jit(solution)/shard_map/cut_own/pallas_call | solution.py:544
  9.6 0.0 collective-permute-done.index_ref.above_ref
  9.6 0.0 copy-start.1
  9.6 0.6 copy-done.1
  10.1 4.7 %cut_above.1.above = f32[4,4,2,128,128]{4,3,2,1,0:T(8,128)} custom-call(s32[12]{0:T(128)} %copy-done.1, f32[4,128,512]{2,1,0:T(8,128)} %phase_ref.3, f32[4,128,512]{2,1,0:T(8,128)} %absorb_ref.3), custom_call_target="tpu_custom_call" | custom-call | bytes 4194304 | tf_op jit(solution)/shard_map/cut_above/pallas_call | solution.py:544
  14.8 35.1 %gather.1 = (f32[2,16,2,128,128]{4,3,2,1,0:T(8,128)}, f32[2,128,128]{2,1,0:T(8,128)}) custom-call(f32[4,4,2,128,128]{4,3,2,1,0:T(8,128)} %cut_own.1.own, f32[4,4,2,128,128]{4,3,2,1,0:T(8,128)} %cut_above.1.above, f32[4,128,128]{2,1,0:T(8,128)} %measured_ref.1), custom_call_target="tpu_custom_call" | custom-call | tf_op jit(solution)/shard_map/gather/pallas_call | solution.py:558
  49.9 69.1 %waves.1 = (f32[4,4,2,128,128]{4,3,2,1,0:T(8,128)}, f32[4,4,2,128,128]{4,3,2,1,0:T(8,128)}) custom-call(s32[12]{0:T(128)} %copy-done, s32[12]{0:T(128)} %copy-done.1, f32[2,16,2,128,128]{4,3,2,1,0:T(8,128)} %get-tuple-element.6.patches, f32[2,128,128]{2,1,0:T(8,128)} %probe_ref.1, f32[4,128,128]{2,1,0:T(8,128)} %measured_ref.1, ...), custom_call_target="tpu_custom_call" | custom-call | tf_op jit(solution)/shard_map/waves/pallas_call | solution.py:579
  119.0 6.4 %place.1 = (f32[4,128,512]{2,1,0:T(8,128)}, f32[4,128,512]{2,1,0:T(8,128)}) custom-call(s32[12]{0:T(128)} %copy-done, s32[12]{0:T(128)} %copy-done.1, f32[4,4,2,128,128]{4,3,2,1,0:T(8,128)} %get-tuple-element.8.own_pieces, f32[4,4,2,128,128]{4,3,2,1,0:T(8,128)} %get-tuple-element.9.above_pieces), custom_call_target="tpu_custom_call" | custom-call | tf_op jit(solution)/shard_map/place/pallas_call | solution.py:597
Async XLA Ops:
  1.4 3.5 %copy-start = (s32[12]{0:T(128)}, s32[12]{0:T(128)S(1)}, u32[]{:S(2)}) copy-start(s32[12]{0:T(128)S(1)} %pad_add_fusion.index_ref.own_ref) | copy-start | bytes 148
  1.4 8.2 %collective-permute-start = (s32[12]{0:T(128)S(1)}, s32[12]{0:T(128)S(1)}, u32[]{:S(2)}, u32[]{:S(2)}) collective-permute-start(s32[12]{0:T(128)S(1)} %pad_add_fusion.index_ref.own_ref), channel_id=1, source_target_pairs={{0,4},{4,8},{8,12},{1,5},{5,9},{9,13},{2,6},{6,10},{10,14},{3,7},{... | collective-permute-start | bytes 152 | tf_op jit(solution)/shard_map/ppermute | solution.py:521
  9.6 0.6 copy-start.1
